TPU v7x, 32 devices: a whole 2x2x4 slice. The times are simulated.
32 devices in a mesh: seq: 8 (over y, x, core), head: 4 (over z).
Axes of the slice: x: 2, y: 2, z: 4, core: 2. Of those that a mesh axis runs over, the one named last changes fastest.
Arguments:
- queries: bfloat16 [8192, 32, 128], P(('seq', 'head')), may hold values from -48 to 48
- keys_in: bfloat16 [8192, 32, 128], P(('seq', 'head')), may hold values from -48 to 48
- values: bfloat16 [8192, 32, 128], P(('seq', 'head')), may hold values from -48 to 48
- cotangent: bfloat16 [8192, 32, 128], P(('seq', 'head')), may hold values from -48 to 48
Outputs:
- attended: bfloat16 [8192, 32, 128], P('seq', 'head')
- grad_queries: bfloat16 [8192, 32, 128], P('seq', 'head')
- grad_keys: bfloat16 [8192, 32, 128], P('seq', 'head')
- grad_values: bfloat16 [8192, 32, 128], P('seq', 'head')
All inputs are finite; a program needn't handle non-finite values.
Results may differ from a plain program's by a relative error of at most 0.01.
Values may be sent and summed in bfloat16 or wider, within the bound.
No kernel may reach another device: no remote copies, remote signals or barrier semaphores. Data moves between devices by JAX's collectives and lax.ppermute only.
A program may use at most 128 MiB of HBM per device.

v0:
```python
import functools

import jax
import jax.numpy as jnp
from jax import lax
from jax.experimental import pallas as pl
from jax.experimental.pallas import tpu as pltpu
from jax.sharding import PartitionSpec as P

BLOCK = 256
OFFSET = 1048576
PAIR = 2
F32 = jnp.float32
BF16 = jnp.bfloat16
ANY = pl.BlockSpec(memory_space=pl.ANY)
HBM = pl.BlockSpec(memory_space=pltpu.HBM)
VMEM = pl.BlockSpec(memory_space=pltpu.VMEM)
SMEM = pl.BlockSpec(memory_space=pltpu.SMEM)
VMEM_BYTES = 32 * 1024 * 1024


def dot(a, b, ca, cb):
    return lax.dot_general(a, b, (((ca,), (cb,)), ((), ())), preferred_element_type=F32)


def params():
    return pltpu.CompilerParams(vmem_limit_bytes=VMEM_BYTES)


def cost(flops, nbytes):
    return pl.CostEstimate(flops=int(flops), bytes_accessed=int(nbytes), transcendentals=0)


def position(first, rows, width):
    index = lax.broadcasted_iota(jnp.int32, (rows, width), 0) + (first + OFFSET + 1)
    return index.astype(F32)


def head_rows(both, wide, h):
    rows, _, width = both.shape
    if h == 0:
        wide[...] = both.reshape(PAIR * rows, width).astype(F32)
    return wide[pl.ds(h, rows, stride=PAIR), :]


def fetch_pairs(where, arrays, held, sems, n, chunk):
    per_group = arrays[0].shape[1] // n
    copies = []
    for d in range(n):
        pair = (where[1] ^ d) * per_group + chunk
        for a, x in enumerate(arrays):
            copies.append(pltpu.make_async_copy(x.at[:, pair], held.at[d, a], sems.at[d, a]))
    for c in copies:
        c.start()
    return copies


def pack_kernel(where, *refs, n, scales, chunk):
    count = len(scales)
    arrays, outs = refs[:count], refs[-3 - n : -3]
    held, wide, sems = refs[-3:]
    rows, width = outs[0].shape[2:]
    copies = fetch_pairs(where, arrays, held, sems, n, chunk)
    for d in range(n):
        for a, scale in enumerate(scales):
            copies[d * count + a].wait()
            for h in range(PAIR):
                part = head_rows(held[d, a], wide, h)
                if scale:
                    part = part / position((where[0] * n + where[1]) * rows, rows, width)
                outs[d][a, h] = part.astype(BF16)


def pack(where, arrays, scales, chunk, n, after):
    rows, _, _, width = arrays[0].shape
    count = len(arrays)
    return pl.pallas_call(
        functools.partial(pack_kernel, n=n, scales=scales, chunk=chunk),
        in_specs=[SMEM] + [HBM] * count + [ANY] * len(after),
        out_specs=[VMEM] * n,
        out_shape=[jax.ShapeDtypeStruct((count, PAIR, rows, width), BF16)] * n,
        scratch_shapes=[
            pltpu.VMEM((n, count, rows, PAIR, width), BF16),
            pltpu.VMEM((PAIR * rows, width), F32),
            pltpu.SemaphoreType.DMA((n, count)),
        ],
        compiler_params=params(),
        cost_estimate=cost(0, 4 * count * n * PAIR * rows * width),
    )(where, *arrays, *after)


def exchange(pieces, n):
    received = list(pieces)
    for d in reversed(range(1, n)):
        received[d] = lax.ppermute(pieces[d], "head", [(j, j ^ d) for j in range(n)])
    return received


def own_rows_kernel(where, *refs, n, chunk):
    arrays, outs = refs[:2], refs[-4 - n : -4]
    held, wide, parts, sems = refs[-4:]
    rows, width = held.shape[2], held.shape[4]
    copies = fetch_pairs(where, arrays, held, sems, n, chunk)
    for d in range(n):
        for a in range(2):
            copies[2 * d + a].wait()
            for h in range(PAIR):
                part = head_rows(held[d, a], wide, h)
                if a == 1:
                    part = part / position((where[0] * n + where[1]) * rows, rows, width)
                parts[a, h] = part.astype(BF16)
        for h in range(PAIR):
            outs[d][h] = dot(parts[0, h], parts[1, h], 0, 0).astype(BF16)


def own_rows_state(where, queries, cotangent, chunk, n, after):
    rows, _, _, width = queries.shape
    return pl.pallas_call(
        functools.partial(own_rows_kernel, n=n, chunk=chunk),
        in_specs=[SMEM] + [HBM] * 2 + [ANY] * len(after),
        out_specs=[VMEM] * n,
        out_shape=[jax.ShapeDtypeStruct((PAIR, width, width), BF16)] * n,
        scratch_shapes=[
            pltpu.VMEM((n, 2, rows, PAIR, width), BF16),
            pltpu.VMEM((PAIR * rows, width), F32),
            pltpu.VMEM((2, PAIR, rows, width), BF16),
            pltpu.SemaphoreType.DMA((n, 2)),
        ],
        compiler_params=params(),
        cost_estimate=cost(2 * n * PAIR * rows * width * width, 8 * n * PAIR * rows * width),
    )(where, queries, cotangent, *after)


def sum_to_group(parts, n):
    parts, bit = list(parts), 1
    while bit < n:
        for d in range(0, n, 2 * bit):
            came = lax.ppermute(parts[d + bit], "head", [(j, j ^ bit) for j in range(n)])
            parts[d] = (parts[d].astype(F32) + came.astype(F32)).astype(BF16)
        bit *= 2
    return parts[0]


def state_kernel(*refs, n, sides):
    for i in range(sides):
        pieces = refs[i * n : (i + 1) * n]
        for h in range(PAIR):
            total = dot(pieces[0][0, h], pieces[0][1, h], 0, 0)
            for d in range(1, n):
                total = total + dot(pieces[d][0, h], pieces[d][1, h], 0, 0)
            refs[-1][i * PAIR + h] = total.astype(BF16)


def shard_state(*sides):
    n = len(sides[0])
    _, _, rows, width = sides[0][0].shape
    count = len(sides)
    return pl.pallas_call(
        functools.partial(state_kernel, n=n, sides=count),
        in_specs=[VMEM] * (n * count),
        out_specs=VMEM,
        out_shape=jax.ShapeDtypeStruct((PAIR * count, width, width), BF16),
        compiler_params=params(),
        cost_estimate=cost(
            2 * count * n * PAIR * rows * width * width, 4 * count * n * PAIR * rows * width
        ),
    )(*[p for side in sides for p in side])


def chunk_kernel(where, *refs, n, block, chunk, slots, n_refs, n_outs, want):
    pieces, kv_states, qg_states = refs[:n_refs], refs[n_refs], refs[n_refs + 1]
    outs = refs[-8 - n_outs : -8]
    held, wide, stage, sums, before_used, after_used, in_sems, out_sems = refs[-8:]
    rows, width = pieces[0].shape[2:]
    row_count = n * rows
    block_count = row_count // block
    shard_count = kv_states.shape[0]
    me, z = where[0], where[1]
    copies = []
    for i, (first, a) in enumerate(slots):
        for d in range(n):
            start = pl.multiple_of((z ^ d) * rows, rows)
            copies.append(
                pltpu.make_async_copy(
                    pieces[first + d].at[a],
                    held.at[i, :, pl.ds(start, rows), :],
                    in_sems.at[i, d],
                )
            )
    for c in copies:
        c.start()

    late = "grads" in want

    def add_shards(j, _):
        for h in range(PAIR):
            sums[0, h] += jnp.where(j < me, kv_states[j, h].astype(F32), 0.0)
            if late:
                sums[1, h] += jnp.where(j > me, qg_states[j, h].astype(F32), 0.0)
        return 0

    sums[...] = jnp.zeros_like(sums)
    lax.fori_loop(0, shard_count, add_shards, 0)
    for c in copies:
        c.wait()

    def span(b):
        return pl.ds(pl.multiple_of(b * block, block), block)

    def add_blocks(i, _):
        last = block_count - 1 - i
        for h in range(PAIR):
            before_used[i, h] = sums[0, h].astype(BF16)
            sums[0, h] += dot(held[0, h, span(i)], held[1, h, span(i)], 0, 0)
            if late:
                after_used[last, h] = sums[1, h].astype(BF16)
                sums[1, h] += dot(held[2, h, span(last)], held[3, h, span(last)], 0, 0)
        return 0

    lax.fori_loop(0, block_count, add_blocks, 0)
    causal = lax.broadcasted_iota(jnp.int32, (block, block), 0) >= lax.broadcasted_iota(
        jnp.int32, (block, block), 1
    )

    def scores(a, b):
        return jnp.where(causal, dot(a, b, 1, 1), 0.0).astype(BF16)

    def out_copy(i, b):
        return pltpu.make_async_copy(
            stage.at[i, span(b)], outs[i].at[span(b), chunk], out_sems.at[i, b]
        )

    def one_block(b, _):
        at = span(b)
        for h in range(PAIR):
            key, value, query = held[0, h, at], held[1, h, at], held[2, h, at]
            prefix = before_used[b, h]
            mine = pl.ds(h, block, stride=PAIR)
            attention = scores(query, key)
            i = 0
            if "attended" in want:
                result = dot(query, prefix, 1, 0) + dot(attention, value, 1, 0)
                wide[0, mine, :] = result / position(me * row_count + b * block, block, width)
                i = 1
            if late:
                grad, suffix = held[3, h, at], after_used[b, h]
                grad_scores = scores(grad, value)
                wide[i, mine, :] = dot(grad, prefix, 1, 1) + dot(grad_scores, key, 1, 0)
                wide[i + 1, mine, :] = dot(value, suffix, 1, 1) + dot(grad_scores, query, 0, 0)
                wide[i + 2, mine, :] = dot(key, suffix, 1, 0) + dot(attention, grad, 0, 0)
        for i in range(n_outs):
            stage[i, at] = wide[i].astype(BF16).reshape(block, PAIR, width)
            out_copy(i, b).start()
        return 0

    lax.fori_loop(0, block_count, one_block, 0)

    def finish(b, _):
        for i in range(n_outs):
            out_copy(i, b).wait()
        return 0

    lax.fori_loop(0, block_count, finish, 0)


def compute_chunk(where, units, slots, kv_states, qg_states, outs, chunk, pair_count, want):
    n = len(units[0])
    _, _, rows, width = units[0][0].shape
    row_count = n * rows
    block = min(BLOCK, row_count)
    block_count = row_count // block
    whole = jax.ShapeDtypeStruct((row_count, pair_count, PAIR, width), BF16)
    n_outs = ("attended" in want) + 3 * ("grads" in want)
    held = [] if outs is None else list(outs)
    pieces = [p for unit in units for p in unit]
    flops = PAIR * row_count * width * 3 * n_outs * (block + width)
    return pl.pallas_call(
        functools.partial(
            chunk_kernel,
            n=n,
            block=block,
            chunk=chunk,
            slots=[(n * u, a) for u, a in slots],
            n_refs=len(pieces),
            n_outs=n_outs,
            want=want,
        ),
        in_specs=[SMEM] + [ANY] * len(pieces) + [VMEM] * 2 + [HBM] * len(held),
        out_specs=[HBM] * n_outs,
        out_shape=[whole] * n_outs,
        scratch_shapes=[
            pltpu.VMEM((len(slots), PAIR, row_count, width), BF16),
            pltpu.VMEM((n_outs, block * PAIR, width), F32),
            pltpu.VMEM((n_outs, row_count, PAIR, width), BF16),
            pltpu.VMEM((2, PAIR, width, width), F32),
            pltpu.VMEM((block_count, PAIR, width, width), BF16),
            pltpu.VMEM((block_count, PAIR, width, width), BF16),
            pltpu.SemaphoreType.DMA((len(slots), n)),
            pltpu.SemaphoreType.DMA((n_outs, block_count)),
        ],
        input_output_aliases={1 + len(pieces) + 2 + i: i for i in range(len(held))},
        compiler_params=params(),
        cost_estimate=cost(flops, 4 * n_outs * PAIR * row_count * width),
    )(where, *pieces, kv_states, qg_states, *held)


def shards(queries, keys_in, values, cotangent):
    n = lax.axis_size("head")
    rows, head_count, width = queries.shape
    pair_count = head_count // PAIR
    per_group = pair_count // n
    last = per_group - 1
    where = jnp.stack([lax.axis_index("seq"), lax.axis_index("head")]).astype(jnp.int32)
    queries, keys_in, values, cotangent = (
        x.reshape(rows, pair_count, PAIR, width) for x in (queries, keys_in, values, cotangent)
    )
    order = []
    for chunk in range(per_group):
        order += [("kv", chunk), ("qg", chunk)]
    order = order[:-1]
    if per_group > 1:
        order[-2], order[-1] = order[-1], order[-2]
    order += [("q", last), ("g", last)]
    content = {
        "kv": ((keys_in, values), (False, False)),
        "qg": ((queries, cotangent), (False, True)),
        "q": ((queries,), (False,)),
        "g": ((cotangent,), (True,)),
    }
    sent, arrived = [], {}
    for unit, (kind, chunk) in enumerate(order):
        after = arrived[order[unit - 2]][1:] if unit >= 2 else []
        arrays, scales = content[kind]
        sent.append(pack(where, arrays, scales, chunk, n, after))
        arrived[kind, chunk] = exchange(sent[-1], n)
    ahead = own_rows_state(where, queries, cotangent, last, n, sent[1][:1])
    last_qg_states = lax.all_gather(sum_to_group(ahead, n), "seq", axis=0)
    last_kv_states = lax.all_gather(shard_state(arrived["kv", last]), "seq", axis=0)
    outs = None
    both = ("attended", "grads")
    for chunk in range(last):
        kv, qg = arrived["kv", chunk], arrived["qg", chunk]
        states = lax.all_gather(shard_state(kv, qg), "seq", axis=0)
        slots = ((0, 0), (0, 1), (1, 0), (1, 1))
        outs = compute_chunk(
            where, (kv, qg), slots, states[:, :PAIR], states[:, PAIR:], outs, chunk, per_group, both
        )
    kv, q, g = arrived["kv", last], arrived["q", last], arrived["g", last]
    attended = compute_chunk(
        where,
        (kv, q),
        ((0, 0), (0, 1), (1, 0)),
        last_kv_states,
        last_qg_states,
        outs and outs[:1],
        last,
        per_group,
        both[:1],
    )
    grads = compute_chunk(
        where,
        (kv, q, g),
        ((0, 0), (0, 1), (1, 0), (2, 0)),
        last_kv_states,
        last_qg_states,
        outs and outs[1:],
        last,
        per_group,
        both[1:],
    )
    return tuple(x.reshape(n * rows, per_group * PAIR, width) for x in (*attended, *grads))


def solution(mesh):
    rows_spec = P(("seq", "head"), None, None)
    heads_spec = P("seq", "head", None)
    return jax.shard_map(
        shards, mesh=mesh, in_specs=(rows_spec,) * 4, out_specs=(heads_spec,) * 4, check_vma=False
    )
```

profile of v0, /device:TPU:0, one launch (start us, length us, event | category | flops | bytes accessed | tf_op | source)
XLA Modules:
  0.0 296.8 jit_solution(6254920743570579950)
XLA Ops:
  7.3 1.6 copy-done.6
  8.9 1.6 copy-done.10
  10.5 2.2 shard_map.81
  12.7 3.1 %collective-permute-start.15 = (bf16[2,2,256,128]{3,2,1,0:T(8,128)(2,1)S(1)}, bf16[2,2,256,128]{3,2,1,0:T(8,128)(2,1)S(1)}, u32[]{:S(2)}, u32[]{:S(2)}) collective-permute-start(bf16[2,2,256,128]{3,2,1,0:T(8,128)(2,1)S(1)} %get-tuple-element.78), channel_id=1, source_target_pairs={{0,1},{1,0},{2,3},{3,2},{4,5},{5,4},{6,7},{7,6},{8,9},{9,8},{10,11... | collective-permute-start | bytes 786440 | tf_op jit(solution)/shard_map/ppermute | solution.py:95
  15.8 2.6 collective-permute-start.16
  18.4 2.3 shard_map.75
  21.7 3.5 %collective-permute-start.1 = (bf16[2,2,256,128]{3,2,1,0:T(8,128)(2,1)S(1)}, bf16[2,2,256,128]{3,2,1,0:T(8,128)(2,1)S(1)}, u32[]{:S(2)}, u32[]{:S(2)}) collective-permute-start(bf16[2,2,256,128]{3,2,1,0:T(8,128)(2,1)S(1)} %get-tuple-element.60), channel_id=1, source_target_pairs={{0,2},{1,3},{2,0},{3,1},{4,6},{5,7},{6,4},{7,5},{8,10},{9,11},{10,... | collective-permute-start | bytes 786440 | tf_op jit(solution)/shard_map/ppermute | solution.py:95
  25.2 2.6 collective-permute-done.15.refs_2_.refs_1_
  27.8 4.6 %collective-permute-start.2 = (bf16[2,2,256,128]{3,2,1,0:T(8,128)(2,1)S(1)}, bf16[2,2,256,128]{3,2,1,0:T(8,128)(2,1)S(1)}, u32[]{:S(2)}, u32[]{:S(2)}) collective-permute-start(bf16[2,2,256,128]{3,2,1,0:T(8,128)(2,1)S(1)} %get-tuple-element.61), channel_id=1, source_target_pairs={{0,3},{1,2},{2,1},{3,0},{4,7},{5,6},{6,5},{7,4},{8,11},{9,10},{10,... | collective-permute-start | bytes 786440 | tf_op jit(solution)/shard_map/ppermute | solution.py:95
  32.4 4.8 %collective-permute-done.16.refs_3_.refs_2_ = bf16[2,2,256,128]{3,2,1,0:T(8,128)(2,1)S(1)} collective-permute-done((bf16[2,2,256,128]{3,2,1,0:T(8,128)(2,1)S(1)}, bf16[2,2,256,128]{3,2,1,0:T(8,128)(2,1)S(1)}, u32[]{:S(2)}, u32[]{:S(2)}) %collective-permute-start.16) | collective-permute-done | bytes 262176 | tf_op jit(solution)/shard_map/ppermute | solution.py:95
  37.2 2.2 collective-permute-done.refs_2_.refs_5_
  39.5 20.2 %collective-permute-done.1.refs_3_.refs_6_ = bf16[2,2,256,128]{3,2,1,0:T(8,128)(2,1)S(1)} collective-permute-done((bf16[2,2,256,128]{3,2,1,0:T(8,128)(2,1)S(1)}, bf16[2,2,256,128]{3,2,1,0:T(8,128)(2,1)S(1)}, u32[]{:S(2)}, u32[]{:S(2)}) %collective-permute-start.1) | collective-permute-done | bytes 262176 | tf_op jit(solution)/shard_map/ppermute | solution.py:95
  59.7 1.1 shard_map.87
  62.3 1.6 copy-done.7
  63.9 1.6 copy-done.11
  65.5 2.2 shard_map.82
  67.8 4.8 %collective-permute-start.18 = (bf16[2,2,256,128]{3,2,1,0:T(8,128)(2,1)S(1)}, bf16[2,2,256,128]{3,2,1,0:T(8,128)(2,1)S(1)}, u32[]{:S(2)}, u32[]{:S(2)}) collective-permute-start(bf16[2,2,256,128]{3,2,1,0:T(8,128)(2,1)S(1)} %get-tuple-element.81), channel_id=1, source_target_pairs={{0,1},{1,0},{2,3},{3,2},{4,5},{5,4},{6,7},{7,6},{8,9},{9,8},{10,11... | collective-permute-start | bytes 786440 | tf_op jit(solution)/shard_map/ppermute | solution.py:95
  73.7 1.4 collective-permute-start.20
  75.1 2.3 shard_map.76
  78.5 2.0 collective-permute-start.4
  80.5 4.4 %collective-permute-done.18.refs_2_.refs_1_ = bf16[2,2,256,128]{3,2,1,0:T(8,128)(2,1)S(1)} collective-permute-done((bf16[2,2,256,128]{3,2,1,0:T(8,128)(2,1)S(1)}, bf16[2,2,256,128]{3,2,1,0:T(8,128)(2,1)S(1)}, u32[]{:S(2)}, u32[]{:S(2)}) %collective-permute-start.18) | collective-permute-done | bytes 262176 | tf_op jit(solution)/shard_map/ppermute | solution.py:95
  84.8 2.8 collective-permute-start.5
  87.6 6.4 %collective-permute-done.19.refs_3_.refs_2_ = bf16[2,2,256,128]{3,2,1,0:T(8,128)(2,1)S(1)} collective-permute-done((bf16[2,2,256,128]{3,2,1,0:T(8,128)(2,1)S(1)}, bf16[2,2,256,128]{3,2,1,0:T(8,128)(2,1)S(1)}, u32[]{:S(2)}, u32[]{:S(2)}) %collective-permute-start.19) | collective-permute-done | bytes 262176 | tf_op jit(solution)/shard_map/ppermute | solution.py:95
  94.0 2.2 collective-permute-done.3.refs_2_.refs_5_
  96.2 20.2 %collective-permute-done.4.refs_3_.refs_6_ = bf16[2,2,256,128]{3,2,1,0:T(8,128)(2,1)S(1)} collective-permute-done((bf16[2,2,256,128]{3,2,1,0:T(8,128)(2,1)S(1)}, bf16[2,2,256,128]{3,2,1,0:T(8,128)(2,1)S(1)}, u32[]{:S(2)}, u32[]{:S(2)}) %collective-permute-start.4) | collective-permute-done | bytes 262176 | tf_op jit(solution)/shard_map/ppermute | solution.py:95
  116.5 1.1 shard_map.86
  119.3 1.6 copy-done.8
  120.9 1.6 copy-done.12
  122.5 2.2 shard_map.83
  124.8 3.7 %collective-permute-start.21 = (bf16[2,2,256,128]{3,2,1,0:T(8,128)(2,1)S(1)}, bf16[2,2,256,128]{3,2,1,0:T(8,128)(2,1)S(1)}, u32[]{:S(2)}, u32[]{:S(2)}) collective-permute-start(bf16[2,2,256,128]{3,2,1,0:T(8,128)(2,1)S(1)} %get-tuple-element.85), channel_id=1, source_target_pairs={{0,1},{1,0},{2,3},{3,2},{4,5},{5,4},{6,7},{7,6},{8,9},{9,8},{10,11... | collective-permute-start | bytes 786440 | tf_op jit(solution)/shard_map/ppermute | solution.py:95
  129.5 1.4 collective-permute-start.23
  130.9 5.1 %collective-permute-done.21.refs_2_.refs_1_ = bf16[2,2,256,128]{3,2,1,0:T(8,128)(2,1)S(1)} collective-permute-done((bf16[2,2,256,128]{3,2,1,0:T(8,128)(2,1)S(1)}, bf16[2,2,256,128]{3,2,1,0:T(8,128)(2,1)S(1)}, u32[]{:S(2)}, u32[]{:S(2)}) %collective-permute-start.21) | collective-permute-done | bytes 262176 | tf_op jit(solution)/shard_map/ppermute | solution.py:95
  136.0 12.9 %collective-permute-done.22.refs_3_.refs_2_ = bf16[2,2,256,128]{3,2,1,0:T(8,128)(2,1)S(1)} collective-permute-done((bf16[2,2,256,128]{3,2,1,0:T(8,128)(2,1)S(1)}, bf16[2,2,256,128]{3,2,1,0:T(8,128)(2,1)S(1)}, u32[]{:S(2)}, u32[]{:S(2)}) %collective-permute-start.22) | collective-permute-done | bytes 262176 | tf_op jit(solution)/shard_map/ppermute | solution.py:95
  148.9 2.3 shard_map.84
  151.2 3.4 %collective-permute-start.24 = (bf16[2,2,256,128]{3,2,1,0:T(8,128)(2,1)S(1)}, bf16[2,2,256,128]{3,2,1,0:T(8,128)(2,1)S(1)}, u32[]{:S(2)}, u32[]{:S(2)}) collective-permute-start(bf16[2,2,256,128]{3,2,1,0:T(8,128)(2,1)S(1)} %get-tuple-element.89), channel_id=1, source_target_pairs={{0,1},{1,0},{2,3},{3,2},{4,5},{5,4},{6,7},{7,6},{8,9},{9,8},{10,11... | collective-permute-start | bytes 786440 | tf_op jit(solution)/shard_map/ppermute | solution.py:95
  154.7 1.4 collective-permute-start.25
  156.0 1.4 collective-permute-start.26
  157.4 4.7 %collective-permute-done.24.refs_5_.refs_1_ = bf16[2,2,256,128]{3,2,1,0:T(8,128)(2,1)S(1)} collective-permute-done((bf16[2,2,256,128]{3,2,1,0:T(8,128)(2,1)S(1)}, bf16[2,2,256,128]{3,2,1,0:T(8,128)(2,1)S(1)}, u32[]{:S(2)}, u32[]{:S(2)}) %collective-permute-start.24) | collective-permute-done | bytes 262176 | tf_op jit(solution)/shard_map/ppermute | solution.py:95
  162.1 12.9 %collective-permute-done.25.refs_6_.refs_2_ = bf16[2,2,256,128]{3,2,1,0:T(8,128)(2,1)S(1)} collective-permute-done((bf16[2,2,256,128]{3,2,1,0:T(8,128)(2,1)S(1)}, bf16[2,2,256,128]{3,2,1,0:T(8,128)(2,1)S(1)}, u32[]{:S(2)}, u32[]{:S(2)}) %collective-permute-start.25) | collective-permute-done | bytes 262176 | tf_op jit(solution)/shard_map/ppermute | solution.py:95
  175.1 1.1 shard_map.85
  179.2 1.6 copy-done.4
  180.8 3.1 %shard_map.80 = (bf16[2,128,128]{2,1,0:T(8,128)(2,1)S(1)}, bf16[2,128,128]{2,1,0:T(8,128)(2,1)S(1)}, bf16[2,128,128]{2,1,0:T(8,128)(2,1)S(1)}, bf16[2,128,128]{2,1,0:T(8,128)(2,1)S(1)}) custom-call(s32[2]{0:T(128)S(1)} %pad_add_fusion.where, bf16[256,16,2,128]{3,2,1,0:T(2,128)(2,1)S(1)} %bitcast.18, bf16[256,16,2,128]{3,2,1,0:T(2,128)(2,1)S(1)} %bitcast.23, ...), custom_call_target="tpu_custom_call" | custom-call | flops 67108864 | bytes 2097152 | tf_op jit(solution)/shard_map/pallas_call | solution.py:118
  183.9 3.4 %collective-permute-start.13 = (bf16[2,128,128]{2,1,0:T(8,128)(2,1)S(1)}, bf16[2,128,128]{2,1,0:T(8,128)(2,1)S(1)}, u32[]{:S(2)}, u32[]{:S(2)}) collective-permute-start(bf16[2,128,128]{2,1,0:T(8,128)(2,1)S(1)} %get-tuple-element.77), channel_id=1, source_target_pairs={{0,1},{1,0},{2,3},{3,2},{4,5},{5,4},{6,7},{7,6},{8,9},{9,8},{10,11... | collective-permute-start | bytes 196616 | tf_op jit(solution)/shard_map/ppermute | solution.py:138
  187.4 2.2 collective-permute-done.13
  189.6 4.5 %collective-permute-start.14 = (bf16[2,128,128]{2,1,0:T(8,128)(2,1)S(1)}, bf16[2,128,128]{2,1,0:T(8,128)(2,1)S(1)}, u32[]{:S(2)}, u32[]{:S(2)}) collective-permute-start(bf16[2,128,128]{2,1,0:T(8,128)(2,1)S(1)} %add_convert_fusion.1), channel_id=1, source_target_pairs={{0,2},{1,3},{2,0},{3,1},{4,6},{5,7},{6,4},{7,5},{8,10},{9,11},{10,... | collective-permute-start | bytes 196616 | tf_op jit(solution)/shard_map/ppermute | solution.py:138
  194.1 2.2 shard_map.77
  196.9 3.8 %collective-permute-start.8 = (bf16[2,2,256,128]{3,2,1,0:T(8,128)(2,1)S(1)}, bf16[2,2,256,128]{3,2,1,0:T(8,128)(2,1)S(1)}, u32[]{:S(2)}, u32[]{:S(2)}) collective-permute-start(bf16[2,2,256,128]{3,2,1,0:T(8,128)(2,1)S(1)} %get-tuple-element.68), channel_id=1, source_target_pairs={{0,3},{1,2},{2,1},{3,0},{4,7},{5,6},{6,5},{7,4},{8,11},{9,10},{10,... | collective-permute-start | bytes 786440 | tf_op jit(solution)/shard_map/ppermute | solution.py:95
  200.8 9.9 %all-gather.1 = bf16[16,128,128]{2,1,0:T(8,128)(2,1)S(1)} all-gather(bf16[2,128,128]{2,1,0:T(8,128)(2,1)S(1)} %add_convert_fusion), channel_id=3, replica_groups=mesh['seq'=8,'head'=4] {'seq'}, dimensions={0}, use_global_device_ids=true | all-gather | bytes 589824 | tf_op jit(solution)/shard_map/all_gather | solution.py:337
  210.7 5.8 %collective-permute-done.7.refs_2_ = bf16[2,2,256,128]{3,2,1,0:T(8,128)(2,1)S(1)} collective-permute-done((bf16[2,2,256,128]{3,2,1,0:T(8,128)(2,1)S(1)}, bf16[2,2,256,128]{3,2,1,0:T(8,128)(2,1)S(1)}, u32[]{:S(2)}, u32[]{:S(2)}) %collective-permute-start.7) | collective-permute-done | bytes 262176 | tf_op jit(solution)/shard_map/ppermute | solution.py:95
  216.5 2.0 shard_map.78
  218.6 4.1 %collective-permute-start.10 = (bf16[1,2,256,128]{3,2,1,0:T(8,128)(2,1)}, bf16[1,2,256,128]{3,2,1,0:T(8,128)(2,1)}, u32[]{:S(2)}, u32[]{:S(2)}) collective-permute-start(bf16[1,2,256,128]{3,2,1,0:T(8,128)(2,1)} %get-tuple-element.71), channel_id=1, source_target_pairs={{0,2},{1,3},{2,0},{3,1},{4,6},{5,7},{6,4},{7,5},{8,10},{9,11},{10,... | collective-permute-start | bytes 393224 | tf_op jit(solution)/shard_map/ppermute | solution.py:95
  222.6 1.9 collective-permute-start.11
  224.9 10.1 %all-gather = bf16[16,128,128]{2,1,0:T(8,128)(2,1)S(1)} all-gather(bf16[2,128,128]{2,1,0:T(8,128)(2,1)S(1)} %shard_map.79), channel_id=2, replica_groups=mesh['seq'=8,'head'=4] {'seq'}, dimensions={0}, use_global_device_ids=true | all-gather | bytes 589824 | tf_op jit(solution)/shard_map/all_gather | solution.py:338
  235.1 2.1 shard_map.92
  238.5 2.0 collective-permute-start.27
  241.0 1.4 fusion
  242.4 9.2 %shard_map.88 = (bf16[1024,4,2,128]{3,2,1,0:T(2,128)(2,1)}, bf16[1024,4,2,128]{3,2,1,0:T(2,128)(2,1)}, bf16[1024,4,2,128]{3,2,1,0:T(2,128)(2,1)}, bf16[1024,4,2,128]{3,2,1,0:T(2,128)(2,1)}) custom-call(s32[2]{0:T(128)S(1)} %pad_add_fusion.where, bf16[2,2,256,128]{3,2,1,0:T(8,128)(2,1)S(1)} %copy-done.69, bf16[2,2,256,128]{3,2,1,0:T(8,128)(2,1)S(1)} %copy-done.45, ...), custom_call_target="tpu_custom_call" | custom-call | flops 1207959552 | bytes 4194304 | tf_op jit(solution)/shard_map/pallas_call | solution.py:277
  251.7 1.4 fusion.1
  253.5 9.3 %shard_map.89 = (bf16[1024,4,2,128]{3,2,1,0:T(2,128)(2,1)}, bf16[1024,4,2,128]{3,2,1,0:T(2,128)(2,1)}, bf16[1024,4,2,128]{3,2,1,0:T(2,128)(2,1)}, bf16[1024,4,2,128]{3,2,1,0:T(2,128)(2,1)}) custom-call(s32[2]{0:T(128)S(1)} %pad_add_fusion.where, ...), custom_call_target="tpu_custom_call", output_to_operand_aliasing={{0}: (11, {}), {1}: (12, {}), {2}: (13, {}), {3}: (14, {})} | custom-call | flops 1207959552 | bytes 4194304 | tf_op jit(solution)/shard_map/pallas_call | solution.py:277
  262.9 1.4 fusion.2
  264.3 2.0 collective-permute-start.29
  266.4 9.3 %shard_map.90 = (bf16[1024,4,2,128]{3,2,1,0:T(2,128)(2,1)}, bf16[1024,4,2,128]{3,2,1,0:T(2,128)(2,1)}, bf16[1024,4,2,128]{3,2,1,0:T(2,128)(2,1)}, bf16[1024,4,2,128]{3,2,1,0:T(2,128)(2,1)}) custom-call(s32[2]{0:T(128)S(1)} %pad_add_fusion.where, ...), custom_call_target="tpu_custom_call", output_to_operand_aliasing={{0}: (11, {}), {1}: (12, {}), {2}: (13, {}), {3}: (14, {})} | custom-call | flops 1207959552 | bytes 4194304 | tf_op jit(solution)/shard_map/pallas_call | solution.py:277
  275.7 6.1 %shard_map.91 = bf16[1024,4,2,128]{3,2,1,0:T(2,128)(2,1)} custom-call(s32[2]{0:T(128)S(1)} %pad_add_fusion.where, bf16[2,2,256,128]{3,2,1,0:T(8,128)(2,1)S(1)} %copy-done.43, bf16[2,2,256,128]{3,2,1,0:T(8,128)(2,1)S(1)} %collective-permute-done.6.refs_1_, ...), custom_call_target="tpu_custom_call", output_to_operand_aliasing={{}: (11, {})} | custom-call | flops 301989888 | bytes 1048576 | tf_op jit(solution)/shard_map/pallas_call | solution.py:277
  281.8 8.4 %shard_map.93 = (bf16[1024,4,2,128]{3,2,1,0:T(2,128)(2,1)}, bf16[1024,4,2,128]{3,2,1,0:T(2,128)(2,1)}, bf16[1024,4,2,128]{3,2,1,0:T(2,128)(2,1)}) custom-call(s32[2]{0:T(128)S(1)} %pad_add_fusion.where, bf16[2,2,256,128]{3,2,1,0:T(8,128)(2,1)S(1)} %copy-done.43, ...), custom_call_target="tpu_custom_call", output_to_operand_aliasing={{0}: (15, {}), {1}: (16, {}), {2}: (17, {})} | custom-call | flops 905969664 | bytes 3145728 | tf_op jit(solution)/shard_map/pallas_call | solution.py:277
  (178 shorter events, 13.8 us)
Async XLA Ops:
  7.2 233.8 %all-gather.13.cloned.1.call-start = ((), (), s32[]{:S(2)}) async-start(), calls=%async_computation.2 | async-start | bytes 1179648 | tf_op jit(solution)/shard_map/all_gather | solution.py:343
  10.5 7.9 %copy-start = (bf16[256,32,128]{2,1,0:T(8,128)(2,1)S(1)}, bf16[256,32,128]{2,1,0:T(8,128)(2,1)}, u32[]{:S(2)}) copy-start(bf16[256,32,128]{2,1,0:T(8,128)(2,1)} %param.4) | copy-start | bytes 6291460
  10.5 7.9 %copy-start.1 = (bf16[256,32,128]{2,1,0:T(8,128)(2,1)S(1)}, bf16[256,32,128]{2,1,0:T(8,128)(2,1)}, u32[]{:S(2)}) copy-start(bf16[256,32,128]{2,1,0:T(8,128)(2,1)} %param.7) | copy-start | bytes 6291460
  12.7 47.0 %copy-start.68 = (bf16[2,2,256,128]{3,2,1,0:T(8,128)(2,1)}, bf16[2,2,256,128]{3,2,1,0:T(8,128)(2,1)S(1)}, u32[]{:S(2)}) copy-start(bf16[2,2,256,128]{3,2,1,0:T(8,128)(2,1)S(1)} %get-tuple-element.94.refs_0_) | copy-start | bytes 786436
  12.7 15.1 %collective-permute-start.15 = (bf16[2,2,256,128]{3,2,1,0:T(8,128)(2,1)S(1)}, bf16[2,2,256,128]{3,2,1,0:T(8,128)(2,1)S(1)}, u32[]{:S(2)}, u32[]{:S(2)}) collective-permute-start(bf16[2,2,256,128]{3,2,1,0:T(8,128)(2,1)S(1)} %get-tuple-element.78), channel_id=1, source_target_pairs={{0,1},{1,0},{2,3},{3,2},{4,5},{5,4},{6,7},{7,6},{8,9},{9,8},{10,11... | collective-permute-start | bytes 786440 | tf_op jit(solution)/shard_map/ppermute | solution.py:95
  15.8 21.4 %collective-permute-start.16 = (bf16[2,2,256,128]{3,2,1,0:T(8,128)(2,1)S(1)}, bf16[2,2,256,128]{3,2,1,0:T(8,128)(2,1)S(1)}, u32[]{:S(2)}, u32[]{:S(2)}) collective-permute-start(bf16[2,2,256,128]{3,2,1,0:T(8,128)(2,1)S(1)} %get-tuple-element.79), channel_id=1, source_target_pairs={{0,2},{1,3},{2,0},{3,1},{4,6},{5,7},{6,4},{7,5},{8,10},{9,11},{10,... | collective-permute-start | bytes 786440 | tf_op jit(solution)/shard_map/ppermute | solution.py:95
  18.4 18.8 %collective-permute-start.17 = (bf16[2,2,256,128]{3,2,1,0:T(8,128)(2,1)S(1)}, bf16[2,2,256,128]{3,2,1,0:T(8,128)(2,1)S(1)}, u32[]{:S(2)}, u32[]{:S(2)}) collective-permute-start(bf16[2,2,256,128]{3,2,1,0:T(8,128)(2,1)S(1)} %get-tuple-element.80), channel_id=1, source_target_pairs={{0,3},{1,2},{2,1},{3,0},{4,7},{5,6},{6,5},{7,4},{8,11},{9,10},{10,... | collective-permute-start | bytes 786440 | tf_op jit(solution)/shard_map/ppermute | solution.py:95
  20.7 18.7 %collective-permute-start = (bf16[2,2,256,128]{3,2,1,0:T(8,128)(2,1)S(1)}, bf16[2,2,256,128]{3,2,1,0:T(8,128)(2,1)S(1)}, u32[]{:S(2)}, u32[]{:S(2)}) collective-permute-start(bf16[2,2,256,128]{3,2,1,0:T(8,128)(2,1)S(1)} %get-tuple-element.59), channel_id=1, source_target_pairs={{0,1},{1,0},{2,3},{3,2},{4,5},{5,4},{6,7},{7,6},{8,9},{9,8},{10,11... | collective-permute-start | bytes 786440 | tf_op jit(solution)/shard_map/ppermute | solution.py:95
  21.7 38.0 %collective-permute-start.1 = (bf16[2,2,256,128]{3,2,1,0:T(8,128)(2,1)S(1)}, bf16[2,2,256,128]{3,2,1,0:T(8,128)(2,1)S(1)}, u32[]{:S(2)}, u32[]{:S(2)}) collective-permute-start(bf16[2,2,256,128]{3,2,1,0:T(8,128)(2,1)S(1)} %get-tuple-element.60), channel_id=1, source_target_pairs={{0,2},{1,3},{2,0},{3,1},{4,6},{5,7},{6,4},{7,5},{8,10},{9,11},{10,... | collective-permute-start | bytes 786440 | tf_op jit(solution)/shard_map/ppermute | solution.py:95
  27.8 39.9 %copy-start.44 = (bf16[2,2,256,128]{3,2,1,0:T(8,128)(2,1)}, bf16[2,2,256,128]{3,2,1,0:T(8,128)(2,1)S(1)}, u32[]{:S(2)}) copy-start(bf16[2,2,256,128]{3,2,1,0:T(8,128)(2,1)S(1)} %collective-permute-done.15.refs_2_.refs_1_) | copy-start | bytes 786436
  27.8 31.9 %collective-permute-start.2 = (bf16[2,2,256,128]{3,2,1,0:T(8,128)(2,1)S(1)}, bf16[2,2,256,128]{3,2,1,0:T(8,128)(2,1)S(1)}, u32[]{:S(2)}, u32[]{:S(2)}) collective-permute-start(bf16[2,2,256,128]{3,2,1,0:T(8,128)(2,1)S(1)} %get-tuple-element.61), channel_id=1, source_target_pairs={{0,3},{1,2},{2,1},{3,0},{4,7},{5,6},{6,5},{7,4},{8,11},{9,10},{10,... | collective-permute-start | bytes 786440 | tf_op jit(solution)/shard_map/ppermute | solution.py:95
  37.2 30.5 %copy-start.46 = (bf16[2,2,256,128]{3,2,1,0:T(8,128)(2,1)}, bf16[2,2,256,128]{3,2,1,0:T(8,128)(2,1)S(1)}, u32[]{:S(2)}) copy-start(bf16[2,2,256,128]{3,2,1,0:T(8,128)(2,1)S(1)} %collective-permute-done.16.refs_3_.refs_2_) | copy-start | bytes 786436
  37.2 30.5 %copy-start.48 = (bf16[2,2,256,128]{3,2,1,0:T(8,128)(2,1)}, bf16[2,2,256,128]{3,2,1,0:T(8,128)(2,1)S(1)}, u32[]{:S(2)}) copy-start(bf16[2,2,256,128]{3,2,1,0:T(8,128)(2,1)S(1)} %collective-permute-done.17.refs_4_.refs_3_) | copy-start | bytes 786436
  39.5 35.6 %copy-start.53 = (bf16[2,2,256,128]{3,2,1,0:T(8,128)(2,1)}, bf16[2,2,256,128]{3,2,1,0:T(8,128)(2,1)S(1)}, u32[]{:S(2)}) copy-start(bf16[2,2,256,128]{3,2,1,0:T(8,128)(2,1)S(1)} %collective-permute-done.refs_2_.refs_5_) | copy-start | bytes 786436
  59.7 15.4 %copy-start.55 = (bf16[2,2,256,128]{3,2,1,0:T(8,128)(2,1)}, bf16[2,2,256,128]{3,2,1,0:T(8,128)(2,1)S(1)}, u32[]{:S(2)}) copy-start(bf16[2,2,256,128]{3,2,1,0:T(8,128)(2,1)S(1)} %collective-permute-done.1.refs_3_.refs_6_) | copy-start | bytes 786436
  62.3 189.5 %all-gather.11.cloned.1.call-start = ((), (), s32[]{:S(2)}) async-start(), calls=%async_computation.1 | async-start | bytes 1179648 | tf_op jit(solution)/shard_map/all_gather | solution.py:343
  65.5 9.6 %copy-start.2 = (bf16[256,32,128]{2,1,0:T(8,128)(2,1)S(1)}, bf16[256,32,128]{2,1,0:T(8,128)(2,1)}, u32[]{:S(2)}) copy-start(bf16[256,32,128]{2,1,0:T(8,128)(2,1)} %param.7) | copy-start | bytes 6291460
  65.5 9.6 %copy-start.58 = (bf16[2,2,256,128]{3,2,1,0:T(8,128)(2,1)S(1)}, bf16[2,2,256,128]{3,2,1,0:T(8,128)(2,1)}, u32[]{:S(2)}) copy-start(bf16[2,2,256,128]{3,2,1,0:T(8,128)(2,1)} %copy-done.57) | copy-start | bytes 786436
  67.8 48.7 %copy-start.60 = (bf16[2,2,256,128]{3,2,1,0:T(8,128)(2,1)}, bf16[2,2,256,128]{3,2,1,0:T(8,128)(2,1)S(1)}, u32[]{:S(2)}) copy-start(bf16[2,2,256,128]{3,2,1,0:T(8,128)(2,1)S(1)} %get-tuple-element.92.refs_0_) | copy-start | bytes 786436
  67.8 17.1 %collective-permute-start.18 = (bf16[2,2,256,128]{3,2,1,0:T(8,128)(2,1)S(1)}, bf16[2,2,256,128]{3,2,1,0:T(8,128)(2,1)S(1)}, u32[]{:S(2)}, u32[]{:S(2)}) collective-permute-start(bf16[2,2,256,128]{3,2,1,0:T(8,128)(2,1)S(1)} %get-tuple-element.81), channel_id=1, source_target_pairs={{0,1},{1,0},{2,3},{3,2},{4,5},{5,4},{6,7},{7,6},{8,9},{9,8},{10,11... | collective-permute-start | bytes 786440 | tf_op jit(solution)/shard_map/ppermute | solution.py:95
  72.6 21.4 %collective-permute-start.19 = (bf16[2,2,256,128]{3,2,1,0:T(8,128)(2,1)S(1)}, bf16[2,2,256,128]{3,2,1,0:T(8,128)(2,1)S(1)}, u32[]{:S(2)}, u32[]{:S(2)}) collective-permute-start(bf16[2,2,256,128]{3,2,1,0:T(8,128)(2,1)S(1)} %get-tuple-element.82), channel_id=1, source_target_pairs={{0,2},{1,3},{2,0},{3,1},{4,6},{5,7},{6,4},{7,5},{8,10},{9,11},{10,... | collective-permute-start | bytes 786440 | tf_op jit(solution)/shard_map/ppermute | solution.py:95
  73.7 20.3 %collective-permute-start.20 = (bf16[2,2,256,128]{3,2,1,0:T(8,128)(2,1)S(1)}, bf16[2,2,256,128]{3,2,1,0:T(8,128)(2,1)S(1)}, u32[]{:S(2)}, u32[]{:S(2)}) collective-permute-start(bf16[2,2,256,128]{3,2,1,0:T(8,128)(2,1)S(1)} %get-tuple-element.83), channel_id=1, source_target_pairs={{0,3},{1,2},{2,1},{3,0},{4,7},{5,6},{6,5},{7,4},{8,11},{9,10},{10,... | collective-permute-start | bytes 786440 | tf_op jit(solution)/shard_map/ppermute | solution.py:95
  77.4 18.9 %collective-permute-start.3 = (bf16[2,2,256,128]{3,2,1,0:T(8,128)(2,1)S(1)}, bf16[2,2,256,128]{3,2,1,0:T(8,128)(2,1)S(1)}, u32[]{:S(2)}, u32[]{:S(2)}) collective-permute-start(bf16[2,2,256,128]{3,2,1,0:T(8,128)(2,1)S(1)} %get-tuple-element.62), channel_id=1, source_target_pairs={{0,1},{1,0},{2,3},{3,2},{4,5},{5,4},{6,7},{7,6},{8,9},{9,8},{10,11... | collective-permute-start | bytes 786440 | tf_op jit(solution)/shard_map/ppermute | solution.py:95
  78.5 38.0 %collective-permute-start.4 = (bf16[2,2,256,128]{3,2,1,0:T(8,128)(2,1)S(1)}, bf16[2,2,256,128]{3,2,1,0:T(8,128)(2,1)S(1)}, u32[]{:S(2)}, u32[]{:S(2)}) collective-permute-start(bf16[2,2,256,128]{3,2,1,0:T(8,128)(2,1)S(1)} %get-tuple-element.63), channel_id=1, source_target_pairs={{0,2},{1,3},{2,0},{3,1},{4,6},{5,7},{6,4},{7,5},{8,10},{9,11},{10,... | collective-permute-start | bytes 786440 | tf_op jit(solution)/shard_map/ppermute | solution.py:95
  84.8 39.9 %copy-start.14 = (bf16[2,2,256,128]{3,2,1,0:T(8,128)(2,1)}, bf16[2,2,256,128]{3,2,1,0:T(8,128)(2,1)S(1)}, u32[]{:S(2)}) copy-start(bf16[2,2,256,128]{3,2,1,0:T(8,128)(2,1)S(1)} %collective-permute-done.18.refs_2_.refs_1_) | copy-start | bytes 786436
  84.8 31.6 %collective-permute-start.5 = (bf16[2,2,256,128]{3,2,1,0:T(8,128)(2,1)S(1)}, bf16[2,2,256,128]{3,2,1,0:T(8,128)(2,1)S(1)}, u32[]{:S(2)}, u32[]{:S(2)}) collective-permute-start(bf16[2,2,256,128]{3,2,1,0:T(8,128)(2,1)S(1)} %get-tuple-element.64), channel_id=1, source_target_pairs={{0,3},{1,2},{2,1},{3,0},{4,7},{5,6},{6,5},{7,4},{8,11},{9,10},{10,... | collective-permute-start | bytes 786440 | tf_op jit(solution)/shard_map/ppermute | solution.py:95
  94.0 30.8 %copy-start.16 = (bf16[2,2,256,128]{3,2,1,0:T(8,128)(2,1)}, bf16[2,2,256,128]{3,2,1,0:T(8,128)(2,1)S(1)}, u32[]{:S(2)}) copy-start(bf16[2,2,256,128]{3,2,1,0:T(8,128)(2,1)S(1)} %collective-permute-done.19.refs_3_.refs_2_) | copy-start | bytes 786436
  94.0 30.8 %copy-start.18 = (bf16[2,2,256,128]{3,2,1,0:T(8,128)(2,1)}, bf16[2,2,256,128]{3,2,1,0:T(8,128)(2,1)S(1)}, u32[]{:S(2)}) copy-start(bf16[2,2,256,128]{3,2,1,0:T(8,128)(2,1)S(1)} %collective-permute-done.20.refs_4_.refs_3_) | copy-start | bytes 786436
  96.2 97.8 %copy-start.20 = (bf16[2,2,256,128]{3,2,1,0:T(8,128)(2,1)}, bf16[2,2,256,128]{3,2,1,0:T(8,128)(2,1)S(1)}, u32[]{:S(2)}) copy-start(bf16[2,2,256,128]{3,2,1,0:T(8,128)(2,1)S(1)} %collective-permute-done.3.refs_2_.refs_5_) | copy-start | bytes 786436
  116.5 77.6 %copy-start.22 = (bf16[2,2,256,128]{3,2,1,0:T(8,128)(2,1)}, bf16[2,2,256,128]{3,2,1,0:T(8,128)(2,1)S(1)}, u32[]{:S(2)}) copy-start(bf16[2,2,256,128]{3,2,1,0:T(8,128)(2,1)S(1)} %collective-permute-done.4.refs_3_.refs_6_) | copy-start | bytes 786436
  119.1 143.7 %all-gather.9.cloned.1.call-start = ((), (), s32[]{:S(2)}) async-start(), calls=%async_computation | async-start | bytes 1179648 | tf_op jit(solution)/shard_map/all_gather | solution.py:343
  122.5 26.4 %copy-start.3 = (bf16[256,32,128]{2,1,0:T(8,128)(2,1)S(1)}, bf16[256,32,128]{2,1,0:T(8,128)(2,1)}, u32[]{:S(2)}) copy-start(bf16[256,32,128]{2,1,0:T(8,128)(2,1)} %param.7) | copy-start | bytes 6291460
  124.8 50.3 %copy-start.64 = (bf16[2,2,256,128]{3,2,1,0:T(8,128)(2,1)}, bf16[2,2,256,128]{3,2,1,0:T(8,128)(2,1)S(1)}, u32[]{:S(2)}) copy-start(bf16[2,2,256,128]{3,2,1,0:T(8,128)(2,1)S(1)} %get-tuple-element.84.refs_0_) | copy-start | bytes 786436
  124.8 11.2 %collective-permute-start.21 = (bf16[2,2,256,128]{3,2,1,0:T(8,128)(2,1)S(1)}, bf16[2,2,256,128]{3,2,1,0:T(8,128)(2,1)S(1)}, u32[]{:S(2)}, u32[]{:S(2)}) collective-permute-start(bf16[2,2,256,128]{3,2,1,0:T(8,128)(2,1)S(1)} %get-tuple-element.85), channel_id=1, source_target_pairs={{0,1},{1,0},{2,3},{3,2},{4,5},{5,4},{6,7},{7,6},{8,9},{9,8},{10,11... | collective-permute-start | bytes 786440 | tf_op jit(solution)/shard_map/ppermute | solution.py:95
  128.4 20.5 %collective-permute-start.22 = (bf16[2,2,256,128]{3,2,1,0:T(8,128)(2,1)S(1)}, bf16[2,2,256,128]{3,2,1,0:T(8,128)(2,1)S(1)}, u32[]{:S(2)}, u32[]{:S(2)}) collective-permute-start(bf16[2,2,256,128]{3,2,1,0:T(8,128)(2,1)S(1)} %get-tuple-element.86), channel_id=1, source_target_pairs={{0,2},{1,3},{2,0},{3,1},{4,6},{5,7},{6,4},{7,5},{8,10},{9,11},{10,... | collective-permute-start | bytes 786440 | tf_op jit(solution)/shard_map/ppermute | solution.py:95
  129.5 19.4 %collective-permute-start.23 = (bf16[2,2,256,128]{3,2,1,0:T(8,128)(2,1)S(1)}, bf16[2,2,256,128]{3,2,1,0:T(8,128)(2,1)S(1)}, u32[]{:S(2)}, u32[]{:S(2)}) collective-permute-start(bf16[2,2,256,128]{3,2,1,0:T(8,128)(2,1)S(1)} %get-tuple-element.87), channel_id=1, source_target_pairs={{0,3},{1,2},{2,1},{3,0},{4,7},{5,6},{6,5},{7,4},{8,11},{9,10},{10,... | collective-permute-start | bytes 786440 | tf_op jit(solution)/shard_map/ppermute | solution.py:95
  136.0 39.1 %copy-start.27 = (bf16[2,2,256,128]{3,2,1,0:T(8,128)(2,1)}, bf16[2,2,256,128]{3,2,1,0:T(8,128)(2,1)S(1)}, u32[]{:S(2)}) copy-start(bf16[2,2,256,128]{3,2,1,0:T(8,128)(2,1)S(1)} %collective-permute-done.21.refs_2_.refs_1_) | copy-start | bytes 786436
  148.9 26.2 %copy-start.29 = (bf16[2,2,256,128]{3,2,1,0:T(8,128)(2,1)}, bf16[2,2,256,128]{3,2,1,0:T(8,128)(2,1)S(1)}, u32[]{:S(2)}) copy-start(bf16[2,2,256,128]{3,2,1,0:T(8,128)(2,1)S(1)} %collective-permute-done.22.refs_3_.refs_2_) | copy-start | bytes 786436
  148.9 26.2 %copy-start.31 = (bf16[2,2,256,128]{3,2,1,0:T(8,128)(2,1)}, bf16[2,2,256,128]{3,2,1,0:T(8,128)(2,1)S(1)}, u32[]{:S(2)}) copy-start(bf16[2,2,256,128]{3,2,1,0:T(8,128)(2,1)S(1)} %collective-permute-done.23.refs_4_.refs_3_) | copy-start | bytes 786436
  151.2 28.0 %copy-start.51 = (bf16[2,2,256,128]{3,2,1,0:T(8,128)(2,1)S(1)}, bf16[2,2,256,128]{3,2,1,0:T(8,128)(2,1)}, u32[]{:S(2)}) copy-start(bf16[2,2,256,128]{3,2,1,0:T(8,128)(2,1)} %copy-done.50) | copy-start | bytes 786436
  151.2 10.9 %collective-permute-start.24 = (bf16[2,2,256,128]{3,2,1,0:T(8,128)(2,1)S(1)}, bf16[2,2,256,128]{3,2,1,0:T(8,128)(2,1)S(1)}, u32[]{:S(2)}, u32[]{:S(2)}) collective-permute-start(bf16[2,2,256,128]{3,2,1,0:T(8,128)(2,1)S(1)} %get-tuple-element.89), channel_id=1, source_target_pairs={{0,1},{1,0},{2,3},{3,2},{4,5},{5,4},{6,7},{7,6},{8,9},{9,8},{10,11... | collective-permute-start | bytes 786440 | tf_op jit(solution)/shard_map/ppermute | solution.py:95
  154.7 20.4 %collective-permute-start.25 = (bf16[2,2,256,128]{3,2,1,0:T(8,128)(2,1)S(1)}, bf16[2,2,256,128]{3,2,1,0:T(8,128)(2,1)S(1)}, u32[]{:S(2)}, u32[]{:S(2)}) collective-permute-start(bf16[2,2,256,128]{3,2,1,0:T(8,128)(2,1)S(1)} %get-tuple-element.90), channel_id=1, source_target_pairs={{0,2},{1,3},{2,0},{3,1},{4,6},{5,7},{6,4},{7,5},{8,10},{9,11},{10,... | collective-permute-start | bytes 786440 | tf_op jit(solution)/shard_map/ppermute | solution.py:95
  156.0 19.0 %collective-permute-start.26 = (bf16[2,2,256,128]{3,2,1,0:T(8,128)(2,1)S(1)}, bf16[2,2,256,128]{3,2,1,0:T(8,128)(2,1)S(1)}, u32[]{:S(2)}, u32[]{:S(2)}) collective-permute-start(bf16[2,2,256,128]{3,2,1,0:T(8,128)(2,1)S(1)} %get-tuple-element.91), channel_id=1, source_target_pairs={{0,3},{1,2},{2,1},{3,0},{4,7},{5,6},{6,5},{7,4},{8,11},{9,10},{10,... | collective-permute-start | bytes 786440 | tf_op jit(solution)/shard_map/ppermute | solution.py:95
  180.8 13.3 %copy-start.9 = (bf16[256,32,128]{2,1,0:T(8,128)(2,1)S(1)}, bf16[256,32,128]{2,1,0:T(8,128)(2,1)}, u32[]{:S(2)}) copy-start(bf16[256,32,128]{2,1,0:T(8,128)(2,1)} %param.5) | copy-start | bytes 6291460
  180.8 13.3 %copy-start.13 = (bf16[256,32,128]{2,1,0:T(8,128)(2,1)S(1)}, bf16[256,32,128]{2,1,0:T(8,128)(2,1)}, u32[]{:S(2)}) copy-start(bf16[256,32,128]{2,1,0:T(8,128)(2,1)} %param.6) | copy-start | bytes 6291460
  180.8 13.3 %copy-start.25 = (bf16[2,2,256,128]{3,2,1,0:T(8,128)(2,1)S(1)}, bf16[2,2,256,128]{3,2,1,0:T(8,128)(2,1)}, u32[]{:S(2)}) copy-start(bf16[2,2,256,128]{3,2,1,0:T(8,128)(2,1)} %copy-done.24) | copy-start | bytes 786436
  183.9 5.7 %collective-permute-start.13 = (bf16[2,128,128]{2,1,0:T(8,128)(2,1)S(1)}, bf16[2,128,128]{2,1,0:T(8,128)(2,1)S(1)}, u32[]{:S(2)}, u32[]{:S(2)}) collective-permute-start(bf16[2,128,128]{2,1,0:T(8,128)(2,1)S(1)} %get-tuple-element.77), channel_id=1, source_target_pairs={{0,1},{1,0},{2,3},{3,2},{4,5},{5,4},{6,7},{7,6},{8,9},{9,8},{10,11... | collective-permute-start | bytes 196616 | tf_op jit(solution)/shard_map/ppermute | solution.py:138
  187.3 13.4 %collective-permute-start.12 = (bf16[2,128,128]{2,1,0:T(8,128)(2,1)S(1)}, bf16[2,128,128]{2,1,0:T(8,128)(2,1)S(1)}, u32[]{:S(2)}, u32[]{:S(2)}) collective-permute-start(bf16[2,128,128]{2,1,0:T(8,128)(2,1)S(1)} %get-tuple-element.75), channel_id=1, source_target_pairs={{0,1},{1,0},{2,3},{3,2},{4,5},{5,4},{6,7},{7,6},{8,9},{9,8},{10,11... | collective-permute-start | bytes 196616 | tf_op jit(solution)/shard_map/ppermute | solution.py:138
  189.6 11.2 %collective-permute-start.14 = (bf16[2,128,128]{2,1,0:T(8,128)(2,1)S(1)}, bf16[2,128,128]{2,1,0:T(8,128)(2,1)S(1)}, u32[]{:S(2)}, u32[]{:S(2)}) collective-permute-start(bf16[2,128,128]{2,1,0:T(8,128)(2,1)S(1)} %add_convert_fusion.1), channel_id=1, source_target_pairs={{0,2},{1,3},{2,0},{3,1},{4,6},{5,7},{6,4},{7,5},{8,10},{9,11},{10,... | collective-permute-start | bytes 196616 | tf_op jit(solution)/shard_map/ppermute | solution.py:138
  196.3 28.6 %copy-start.42 = (bf16[2,2,256,128]{3,2,1,0:T(8,128)(2,1)}, bf16[2,2,256,128]{3,2,1,0:T(8,128)(2,1)S(1)}, u32[]{:S(2)}) copy-start(bf16[2,2,256,128]{3,2,1,0:T(8,128)(2,1)S(1)} %get-tuple-element.65.refs_0_) | copy-start | bytes 786436
  196.3 14.4 %collective-permute-start.6 = (bf16[2,2,256,128]{3,2,1,0:T(8,128)(2,1)S(1)}, bf16[2,2,256,128]{3,2,1,0:T(8,128)(2,1)S(1)}, u32[]{:S(2)}, u32[]{:S(2)}) collective-permute-start(bf16[2,2,256,128]{3,2,1,0:T(8,128)(2,1)S(1)} %get-tuple-element.66), channel_id=1, source_target_pairs={{0,1},{1,0},{2,3},{3,2},{4,5},{5,4},{6,7},{7,6},{8,9},{9,8},{10,11... | collective-permute-start | bytes 786440 | tf_op jit(solution)/shard_map/ppermute | solution.py:95
  196.4 20.1 %collective-permute-start.7 = (bf16[2,2,256,128]{3,2,1,0:T(8,128)(2,1)S(1)}, bf16[2,2,256,128]{3,2,1,0:T(8,128)(2,1)S(1)}, u32[]{:S(2)}, u32[]{:S(2)}) collective-permute-start(bf16[2,2,256,128]{3,2,1,0:T(8,128)(2,1)S(1)} %get-tuple-element.67), channel_id=1, source_target_pairs={{0,2},{1,3},{2,0},{3,1},{4,6},{5,7},{6,4},{7,5},{8,10},{9,11},{10,... | collective-permute-start | bytes 786440 | tf_op jit(solution)/shard_map/ppermute | solution.py:95
  196.9 19.6 %collective-permute-start.8 = (bf16[2,2,256,128]{3,2,1,0:T(8,128)(2,1)S(1)}, bf16[2,2,256,128]{3,2,1,0:T(8,128)(2,1)S(1)}, u32[]{:S(2)}, u32[]{:S(2)}) collective-permute-start(bf16[2,2,256,128]{3,2,1,0:T(8,128)(2,1)S(1)} %get-tuple-element.68), channel_id=1, source_target_pairs={{0,3},{1,2},{2,1},{3,0},{4,7},{5,6},{6,5},{7,4},{8,11},{9,10},{10,... | collective-permute-start | bytes 786440 | tf_op jit(solution)/shard_map/ppermute | solution.py:95
  210.7 24.3 %copy-start.5 = (bf16[256,32,128]{2,1,0:T(8,128)(2,1)S(1)}, bf16[256,32,128]{2,1,0:T(8,128)(2,1)}, u32[]{:S(2)}) copy-start(bf16[256,32,128]{2,1,0:T(8,128)(2,1)} %param.7) | copy-start | bytes 6291460
  210.7 24.3 %copy-start.34 = (bf16[2,2,256,128]{3,2,1,0:T(8,128)(2,1)S(1)}, bf16[2,2,256,128]{3,2,1,0:T(8,128)(2,1)}, u32[]{:S(2)}) copy-start(bf16[2,2,256,128]{3,2,1,0:T(8,128)(2,1)} %copy-done.33) | copy-start | bytes 786436
  210.7 24.3 %copy-start.37 = (bf16[2,2,256,128]{3,2,1,0:T(8,128)(2,1)S(1)}, bf16[2,2,256,128]{3,2,1,0:T(8,128)(2,1)}, u32[]{:S(2)}) copy-start(bf16[2,2,256,128]{3,2,1,0:T(8,128)(2,1)} %copy-done.36) | copy-start | bytes 786436
  210.7 24.3 %copy-start.40 = (bf16[2,2,256,128]{3,2,1,0:T(8,128)(2,1)S(1)}, bf16[2,2,256,128]{3,2,1,0:T(8,128)(2,1)}, u32[]{:S(2)}) copy-start(bf16[2,2,256,128]{3,2,1,0:T(8,128)(2,1)} %copy-done.39) | copy-start | bytes 786436
  218.6 45.7 %collective-permute-start.10 = (bf16[1,2,256,128]{3,2,1,0:T(8,128)(2,1)}, bf16[1,2,256,128]{3,2,1,0:T(8,128)(2,1)}, u32[]{:S(2)}, u32[]{:S(2)}) collective-permute-start(bf16[1,2,256,128]{3,2,1,0:T(8,128)(2,1)} %get-tuple-element.71), channel_id=1, source_target_pairs={{0,2},{1,3},{2,0},{3,1},{4,6},{5,7},{6,4},{7,5},{8,10},{9,11},{10,... | collective-permute-start | bytes 393224 | tf_op jit(solution)/shard_map/ppermute | solution.py:95
  222.6 53.0 %collective-permute-start.11 = (bf16[1,2,256,128]{3,2,1,0:T(8,128)(2,1)}, bf16[1,2,256,128]{3,2,1,0:T(8,128)(2,1)}, u32[]{:S(2)}, u32[]{:S(2)}) collective-permute-start(bf16[1,2,256,128]{3,2,1,0:T(8,128)(2,1)} %get-tuple-element.72), channel_id=1, source_target_pairs={{0,3},{1,2},{2,1},{3,0},{4,7},{5,6},{6,5},{7,4},{8,11},{9,10},{10,... | collective-permute-start | bytes 393224 | tf_op jit(solution)/shard_map/ppermute | solution.py:95
  224.5 51.1 %collective-permute-start.9 = (bf16[1,2,256,128]{3,2,1,0:T(8,128)(2,1)}, bf16[1,2,256,128]{3,2,1,0:T(8,128)(2,1)}, u32[]{:S(2)}, u32[]{:S(2)}) collective-permute-start(bf16[1,2,256,128]{3,2,1,0:T(8,128)(2,1)} %get-tuple-element.70), channel_id=1, source_target_pairs={{0,1},{1,0},{2,3},{3,2},{4,5},{5,4},{6,7},{7,6},{8,9},{9,8},{10,11... | collective-permute-start | bytes 393224 | tf_op jit(solution)/shard_map/ppermute | solution.py:95
  238.5 43.3 %collective-permute-start.27 = (bf16[1,2,256,128]{3,2,1,0:T(8,128)(2,1)}, bf16[1,2,256,128]{3,2,1,0:T(8,128)(2,1)}, u32[]{:S(2)}, u32[]{:S(2)}) collective-permute-start(bf16[1,2,256,128]{3,2,1,0:T(8,128)(2,1)} %get-tuple-element.105), channel_id=1, source_target_pairs={{0,1},{1,0},{2,3},{3,2},{4,5},{5,4},{6,7},{7,6},{8,9},{9,8},{10,11... | collective-permute-start | bytes 393224 | tf_op jit(solution)/shard_map/ppermute | solution.py:95
  240.5 41.3 %collective-permute-start.28 = (bf16[1,2,256,128]{3,2,1,0:T(8,128)(2,1)}, bf16[1,2,256,128]{3,2,1,0:T(8,128)(2,1)}, u32[]{:S(2)}, u32[]{:S(2)}) collective-permute-start(bf16[1,2,256,128]{3,2,1,0:T(8,128)(2,1)} %get-tuple-element.106), channel_id=1, source_target_pairs={{0,2},{1,3},{2,0},{3,1},{4,6},{5,7},{6,4},{7,5},{8,10},{9,11},{10,... | collective-permute-start | bytes 393224 | tf_op jit(solution)/shard_map/ppermute | solution.py:95
  264.3 17.5 %collective-permute-start.29 = (bf16[1,2,256,128]{3,2,1,0:T(8,128)(2,1)}, bf16[1,2,256,128]{3,2,1,0:T(8,128)(2,1)S(1)}, u32[]{:S(2)}, u32[]{:S(2)}) collective-permute-start(bf16[1,2,256,128]{3,2,1,0:T(8,128)(2,1)} %copy-done.72), channel_id=1, source_target_pairs={{0,3},{1,2},{2,1},{3,0},{4,7},{5,6},{6,5},{7,4},{8,11},{9,10},{10,... | collective-permute-start | bytes 393224 | tf_op jit(solution)/shard_map/ppermute | solution.py:95
  266.3 9.3 %copy-start.43 = (bf16[2,2,256,128]{3,2,1,0:T(8,128)(2,1)S(1)}, bf16[2,2,256,128]{3,2,1,0:T(8,128)(2,1)}, u32[]{:S(2)}) copy-start(bf16[2,2,256,128]{3,2,1,0:T(8,128)(2,1)} %copy-done.42) | copy-start | bytes 786436
  (42 other events, 112.1 us)
Sparse Core Ops, SparseCore 0:
  62.4 26.8 all-gather.12
  119.2 25.7 all-gather.10
  179.3 26.4 all-gather.8
where the time goes:
time: 297 us
  waiting for transfers between devices  107 us (36%)
  Pallas kernels  69 us (23%)
  starting transfers between devices  63.3 us (21%)
  local copies, waits for them, and re-layouts  22.8 us (8%)
  blocking collectives  20 us (7%)
  between operations  14.6 us (5%)
    ppermute x27, waiting for transfers between devices, exchange(): lax.ppermute(pieces[d], 'head', [(j, j ^ d) for j in range(n)])  105 us
    ppermute x27, starting transfers between devices, exchange(): lax.ppermute(pieces[d], 'head', [(j, j ^ d) for j in range(n)])  55 us
    pallas_call x5, Pallas kernels, compute_chunk(): pl.pallas_call(functools.partial(chunk_kernel, n=n, block=block, chunk=ch...  42.3 us
    pallas_call x9, Pallas kernels, pack(): pl.pallas_call(functools.partial(pack_kernel, n=n, scales=scales, chunk=c...  19.9 us
    unnamed x146, local copies, waits for them, and re-layouts  18.6 us
    all_gather x1, blocking collectives, shards(): lax.all_gather(shard_state(arrived['kv', last]), 'seq', axis=0)  10.1 us
    all_gather x1, blocking collectives, shards(): last_qg_states = lax.all_gather(sum_to_group(ahead, n), 'seq', axis=0)  9.88 us
    ppermute x3, starting transfers between devices, sum_to_group(): lax.ppermute(parts[d + bit], 'head', [(j, j ^ bit) for j in range(n)])  7.95 us
  transfers between devices with their start and end apart: 33, of which 14 were waited for; matrix products, arithmetic and copies ran while one was open for 1% of the time, Pallas kernels for 19%

commit v1 on v0

v1 whole, which is shorter than its diff:
```python
import functools

import jax
import jax.numpy as jnp
from jax import lax
from jax.experimental import pallas as pl
from jax.experimental.pallas import tpu as pltpu
from jax.sharding import PartitionSpec as P

BLOCK = 256
OFFSET = 1048576
PAIR = 2
K, V, Q, G = range(4)
F32 = jnp.float32
BF16 = jnp.bfloat16
ANY = pl.BlockSpec(memory_space=pl.ANY)
HBM = pl.BlockSpec(memory_space=pltpu.HBM)
VMEM = pl.BlockSpec(memory_space=pltpu.VMEM)
SMEM = pl.BlockSpec(memory_space=pltpu.SMEM)
VMEM_BYTES = 32 * 1024 * 1024
TOKEN = jax.ShapeDtypeStruct((8, 128), F32)


def dot(a, b, ca, cb):
    return lax.dot_general(a, b, (((ca,), (cb,)), ((), ())), preferred_element_type=F32)


def params():
    return pltpu.CompilerParams(vmem_limit_bytes=VMEM_BYTES)


def cost(flops, nbytes):
    return pl.CostEstimate(flops=int(flops), bytes_accessed=int(nbytes), transcendentals=0)


def position(first, rows, width):
    index = lax.broadcasted_iota(jnp.int32, (rows, width), 0) + (first + OFFSET + 1)
    return index.astype(F32)


def each(count, body):
    def step(i, _):
        body(i)
        return 0

    lax.fori_loop(0, count, step, 0)


def fetch_pairs(where, arrays, items, held, sems, n):
    per_group = arrays[0].shape[1] // n
    copies = []
    for d in range(n):
        for i, (a, chunk) in enumerate(items):
            pair = (where[1] ^ d) * per_group + chunk
            copies.append(
                pltpu.make_async_copy(arrays[a].at[:, pair], held.at[d, i], sems.at[d, i])
            )
    for c in copies:
        c.start()
    for c in copies:
        c.wait()


def split_heads(where, items, held, wide, put, d, n):
    rows, width = held.shape[2], held.shape[4]
    plain = sum(a != G for a, _ in items)

    def some(first, count, scale):
        def one(j):
            i = first + j
            wide[...] = held[d, i].reshape(PAIR * rows, width).astype(F32)
            for h in range(PAIR):
                part = wide[pl.ds(h, rows, stride=PAIR), :]
                if scale:
                    part = part / position((where[0] * n + where[1]) * rows, rows, width)
                put(i, h, part.astype(BF16))

        if count:
            each(count, one)

    some(0, plain, False)
    some(plain, len(items) - plain, True)


def pack_kernel(where, *refs, n, items):
    arrays, outs = refs[:4], refs[-5 - n : -5]
    held, wide, staged, sems, out_sems = refs[-5:]
    fetch_pairs(where, arrays, items, held, sems, n)

    def one(d):
        def put(i, h, part):
            staged[d, i, h] = part

        split_heads(where, items, held, wide, put, d, n)

    each(n, one)
    copies = [pltpu.make_async_copy(staged.at[d], outs[d], out_sems.at[d]) for d in range(n)]
    for c in copies:
        c.start()
    for c in copies:
        c.wait()


def pack(where, arrays, items, n, after):
    rows, _, _, width = arrays[0].shape
    count = len(items)
    return pl.pallas_call(
        functools.partial(pack_kernel, n=n, items=items),
        in_specs=[SMEM] + [HBM] * 4 + [ANY] * len(after),
        out_specs=[VMEM] * n,
        out_shape=[jax.ShapeDtypeStruct((count, PAIR, rows, width), BF16)] * n,
        scratch_shapes=[
            pltpu.VMEM((n, count, rows, PAIR, width), BF16),
            pltpu.VMEM((PAIR * rows, width), F32),
            pltpu.VMEM((n, count, PAIR, rows, width), BF16),
            pltpu.SemaphoreType.DMA((n, count)),
            pltpu.SemaphoreType.DMA((n,)),
        ],
        compiler_params=params(),
        cost_estimate=cost(0, 4 * count * n * PAIR * rows * width),
    )(where, *arrays, *after)


def exchange(pieces, n):
    received = list(pieces)
    for d in reversed(range(1, n)):
        received[d] = lax.ppermute(pieces[d], "head", [(j, j ^ d) for j in range(n)])
    return received


def own_rows_kernel(where, *refs, n, items):
    arrays, outs = refs[:4], refs[-5 - n : -5]
    held, wide, parts, totals, sems = refs[-5:]
    fetch_pairs(where, arrays, items, held, sems, n)

    def one(d):
        def put(i, h, part):
            parts[i, h] = part

        split_heads(where, items, held, wide, put, d, n)
        for h in range(PAIR):
            totals[d, h] = dot(parts[0, h], parts[1, h], 0, 0).astype(BF16)
            totals[d, PAIR + h] = dot(parts[2, h], parts[3, h], 0, 0).astype(BF16)

    each(n, one)
    for d in range(n):
        outs[d][...] = totals[d]


def own_rows_states(where, arrays, chunk, n, after):
    rows, _, _, width = arrays[0].shape
    items = [(K, chunk), (V, chunk), (Q, chunk), (G, chunk)]
    return pl.pallas_call(
        functools.partial(own_rows_kernel, n=n, items=items),
        in_specs=[SMEM] + [HBM] * 4 + [ANY] * len(after),
        out_specs=[VMEM] * n,
        out_shape=[jax.ShapeDtypeStruct((2 * PAIR, width, width), BF16)] * n,
        scratch_shapes=[
            pltpu.VMEM((n, 4, rows, PAIR, width), BF16),
            pltpu.VMEM((PAIR * rows, width), F32),
            pltpu.VMEM((4, PAIR, rows, width), BF16),
            pltpu.VMEM((n, 2 * PAIR, width, width), BF16),
            pltpu.SemaphoreType.DMA((n, 4)),
        ],
        compiler_params=params(),
        cost_estimate=cost(4 * n * PAIR * rows * width * width, 16 * n * PAIR * rows * width),
    )(where, *arrays, *after)


def sum_to_group(parts, n):
    parts, bit = list(parts), 1
    while bit < n:
        for d in range(0, n, 2 * bit):
            came = lax.ppermute(parts[d + bit], "head", [(j, j ^ bit) for j in range(n)])
            parts[d] = (parts[d].astype(F32) + came.astype(F32)).astype(BF16)
        bit *= 2
    return parts[0]


def state_kernel(*refs, n, sides):
    out = refs[-1]

    def one(h):
        for i, (first, a, second, b) in enumerate(sides):
            total = dot(refs[first][a, h], refs[second][b, h], 0, 0)
            for d in range(1, n):
                total = total + dot(refs[first + d][a, h], refs[second + d][b, h], 0, 0)
            out[i * PAIR + h] = total.astype(BF16)

    each(PAIR, one)


def shard_states(units, sides, after):
    n = len(units[0])
    _, _, rows, width = units[0][0].shape
    count = len(sides)
    return pl.pallas_call(
        functools.partial(state_kernel, n=n, sides=[(n * u, a, n * w, b) for u, a, w, b in sides]),
        in_specs=[VMEM] * (n * len(units)) + [ANY] * len(after),
        out_specs=VMEM,
        out_shape=jax.ShapeDtypeStruct((PAIR * count, width, width), BF16),
        compiler_params=params(),
        cost_estimate=cost(
            2 * count * n * PAIR * rows * width * width, 4 * count * n * PAIR * rows * width
        ),
    )(*[p for unit in units for p in unit], *after)


def place_rows(z, pieces, places, held, first, sems, n):
    rows = pieces[0].shape[2]
    copies = []
    for i, (at, a) in enumerate(places):
        for d in range(n):
            start = pl.multiple_of((z ^ d) * rows, rows)
            copies.append(
                pltpu.make_async_copy(
                    pieces[at + d].at[a],
                    held.at[first + i, :, pl.ds(start, rows), :],
                    sems.at[i, d],
                )
            )
    for c in copies:
        c.start()
    return copies


def masks(block):
    row = lax.broadcasted_iota(jnp.int32, (block, block), 0)
    column = lax.broadcasted_iota(jnp.int32, (block, block), 1)
    return row >= column, row <= column


def scores(a, b, mask):
    return jnp.where(mask, dot(a, b, 1, 1), 0.0).astype(BF16)


def span(b, block):
    return pl.ds(b * block if isinstance(b, int) else pl.multiple_of(b * block, block), block)


def add_shards(me, kv_states, qg_states, sums):
    sums[...] = jnp.zeros_like(sums)

    def one(j):
        for h in range(PAIR):
            sums[0, h] += jnp.where(j < me, kv_states[j, h].astype(F32), 0.0)
            sums[1, h] += jnp.where(j > me, qg_states[j, h].astype(F32), 0.0)

    each(kv_states.shape[0], one)


def out_copy(stage, outs, sems, i, b, block, chunk):
    at = span(b, block)
    return pltpu.make_async_copy(stage.at[i, at], outs[i].at[at, chunk], sems.at[i, b])


def send_block(wide, stage, outs, sems, b, block, chunk, width):
    for i in range(len(outs)):
        stage[i, span(b, block)] = wide[i].astype(BF16).reshape(block, PAIR, width)
        out_copy(stage, outs, sems, i, b, block, chunk).start()


def chunk_kernel(where, *refs, n, block, chunk, slots, n_pieces):
    pieces, kv_states, qg_states = refs[:n_pieces], refs[n_pieces], refs[n_pieces + 1]
    outs, token = refs[-13:-9], refs[-9]
    held, wide, stage, sums, before_used, after_used, in_sems, out_sems = refs[-8:]
    row_count, width = held.shape[2:]
    block_count = row_count // block
    me, z = where[0], where[1]
    copies = place_rows(z, pieces, slots, held, 0, in_sems, n)
    add_shards(me, kv_states, qg_states, sums)
    for c in copies:
        c.wait()

    def add_blocks(i):
        last = block_count - 1 - i
        first_at, last_at = span(i, block), span(last, block)
        for h in range(PAIR):
            before_used[i, h] = sums[0, h].astype(BF16)
            sums[0, h] += dot(held[K, h, first_at], held[V, h, first_at], 0, 0)
            after_used[last, h] = sums[1, h].astype(BF16)
            sums[1, h] += dot(held[Q, h, last_at], held[G, h, last_at], 0, 0)

    each(block_count, add_blocks)
    lower, upper = masks(block)

    def one_block(b):
        at = span(b, block)
        for h in range(PAIR):
            key, value = held[K, h, at], held[V, h, at]
            query, grad = held[Q, h, at], held[G, h, at]
            prefix, suffix = before_used[b, h], after_used[b, h]
            mine = pl.ds(h, block, stride=PAIR)
            attention, attention_t = scores(query, key, lower), scores(key, query, upper)
            grad_scores, grad_scores_t = scores(grad, value, lower), scores(value, grad, upper)
            result = dot(query, prefix, 1, 0) + dot(attention, value, 1, 0)
            wide[0, mine, :] = result / position(me * row_count + b * block, block, width)
            wide[1, mine, :] = dot(grad, prefix, 1, 1) + dot(grad_scores, key, 1, 0)
            wide[2, mine, :] = dot(value, suffix, 1, 1) + dot(grad_scores_t, query, 1, 0)
            wide[3, mine, :] = dot(key, suffix, 1, 0) + dot(attention_t, grad, 1, 0)
        send_block(wide, stage, outs, out_sems, b, block, chunk, width)

    each(block_count, one_block)
    token[...] = jnp.zeros_like(token)

    def finish(b):
        for i in range(4):
            out_copy(stage, outs, out_sems, i, b, block, chunk).wait()

    each(block_count, finish)


def compute_chunk(where, units, slots, kv_states, qg_states, outs, chunk, pair_count, after):
    n = len(units[0])
    _, _, rows, width = units[0][0].shape
    row_count = n * rows
    block = min(BLOCK, row_count)
    block_count = row_count // block
    whole = jax.ShapeDtypeStruct((row_count, pair_count, PAIR, width), BF16)
    held = [] if outs is None else list(outs)
    pieces = [p for unit in units for p in unit]
    result = pl.pallas_call(
        functools.partial(
            chunk_kernel,
            n=n,
            block=block,
            chunk=chunk,
            slots=[(n * u, a) for u, a in slots],
            n_pieces=len(pieces),
        ),
        in_specs=[SMEM] + [ANY] * len(pieces) + [VMEM] * 2 + [HBM] * len(held) + [ANY] * len(after),
        out_specs=[HBM] * 4 + [VMEM],
        out_shape=[whole] * 4 + [TOKEN],
        scratch_shapes=[
            pltpu.VMEM((4, PAIR, row_count, width), BF16),
            pltpu.VMEM((4, block * PAIR, width), F32),
            pltpu.VMEM((4, row_count, PAIR, width), BF16),
            pltpu.VMEM((2, PAIR, width, width), F32),
            pltpu.VMEM((block_count, PAIR, width, width), BF16),
            pltpu.VMEM((block_count, PAIR, width, width), BF16),
            pltpu.SemaphoreType.DMA((4, n)),
            pltpu.SemaphoreType.DMA((4, block_count)),
        ],
        input_output_aliases={1 + len(pieces) + 2 + i: i for i in range(len(held))},
        compiler_params=params(),
        cost_estimate=cost(
            PAIR * row_count * width * 14 * (block + width), 16 * PAIR * row_count * width
        ),
    )(where, *pieces, kv_states, qg_states, *held, *after)
    return result[:4], result[4]


def early_kernel(where, *refs, n, block, chunk):
    pieces, kv_states, qg_states = refs[:n], refs[n], refs[n + 1]
    outs, (held, attention_t, query_t, before_used, sums) = refs[-10:-9], refs[-9:-4]
    wide, stage, in_sems, out_sems = refs[-4:]
    row_count, width = held.shape[2:]
    block_count = row_count // block
    me, z = where[0], where[1]
    copies = place_rows(z, pieces, [(0, K), (0, V), (0, Q)], held, 0, in_sems, n)
    add_shards(me, kv_states, qg_states, sums)
    for c in copies:
        c.wait()
    lower, upper = masks(block)

    def one_block(b):
        at = span(b, block)
        for h in range(PAIR):
            key, value, query = held[K, h, at], held[V, h, at], held[Q, h, at]
            prefix = sums[0, h].astype(BF16)
            before_used[b, h] = prefix
            sums[0, h] += dot(key, value, 0, 0)
            attention_t[b, h] = scores(key, query, upper)
            query_t[b, h] = query.T
            result = dot(query, prefix, 1, 0) + dot(scores(query, key, lower), value, 1, 0)
            wide[0, pl.ds(h, block, stride=PAIR), :] = result / position(
                me * row_count + b * block, block, width
            )
        send_block(wide, stage, outs, out_sems, b, block, chunk, width)

    each(block_count, one_block)
    each(block_count, lambda b: out_copy(stage, outs, out_sems, 0, b, block, chunk).wait())


def late_kernel(where, *refs, n, block, chunk):
    pieces, (held, attention_t, query_t, before_used, sums) = refs[:n], refs[n : n + 5]
    outs = refs[-8:-5]
    grads, wide, stage, in_sems, out_sems = refs[-5:]
    row_count, width = held.shape[2:]
    block_count = row_count // block
    copies = place_rows(where[1], pieces, [(0, 0)], grads, 0, in_sems, n)
    lower, upper = masks(block)
    after = [sums[1, h] for h in range(PAIR)]
    for c in copies:
        c.wait()
    for b in reversed(range(block_count)):
        at = span(b, block)
        turn = wide.at[b % 2]
        for h in range(PAIR):
            key, value, query = held[K, h, at], held[V, h, at], held[Q, h, at]
            grad = grads[0, h, at]
            prefix, suffix = before_used[b, h], after[h].astype(BF16)
            mine = pl.ds(h, block, stride=PAIR)
            grad_scores, grad_scores_t = scores(grad, value, lower), scores(value, grad, upper)
            turn[0, mine, :] = dot(grad, prefix, 1, 1) + dot(grad_scores, key, 1, 0)
            turn[1, mine, :] = dot(value, suffix, 1, 1) + dot(grad_scores_t, query, 1, 0)
            turn[2, mine, :] = dot(key, suffix, 1, 0) + dot(attention_t[b, h], grad, 1, 0)
            if b:
                after[h] = after[h] + dot(query_t[b, h], grad, 1, 0)
        send_block(turn, stage, outs, out_sems, b, block, chunk, width)
    for b in range(block_count):
        for i in range(3):
            out_copy(stage, outs, out_sems, i, b, block, chunk).wait()


def last_chunk(where, kvq, g, kv_states, qg_states, outs, chunk, pair_count, after):
    n = len(kvq)
    _, _, rows, width = kvq[0].shape
    row_count = n * rows
    block = min(BLOCK, row_count)
    block_count = row_count // block
    whole = jax.ShapeDtypeStruct((row_count, pair_count, PAIR, width), BF16)
    held = [] if outs is None else list(outs)
    kept = [
        jax.ShapeDtypeStruct((3, PAIR, row_count, width), BF16),
        jax.ShapeDtypeStruct((block_count, PAIR, block, block), BF16),
        jax.ShapeDtypeStruct((block_count, PAIR, width, block), BF16),
        jax.ShapeDtypeStruct((block_count, PAIR, width, width), BF16),
        jax.ShapeDtypeStruct((2, PAIR, width, width), F32),
    ]
    flops = PAIR * row_count * width * (block + width)
    early = pl.pallas_call(
        functools.partial(early_kernel, n=n, block=block, chunk=chunk),
        in_specs=[SMEM] + [ANY] * n + [VMEM] * 2 + [HBM] * len(held[:1]) + [ANY] * len(after),
        out_specs=[HBM] + [VMEM] * 5,
        out_shape=[whole] + kept,
        scratch_shapes=[
            pltpu.VMEM((1, block * PAIR, width), F32),
            pltpu.VMEM((1, row_count, PAIR, width), BF16),
            pltpu.SemaphoreType.DMA((3, n)),
            pltpu.SemaphoreType.DMA((1, block_count)),
        ],
        input_output_aliases={1 + n + 2: 0} if held else {},
        compiler_params=params(),
        cost_estimate=cost(6 * flops, 8 * PAIR * row_count * width),
    )(where, *kvq, kv_states, qg_states, *held[:1], *after)
    late = pl.pallas_call(
        functools.partial(late_kernel, n=n, block=block, chunk=chunk),
        in_specs=[SMEM] + [ANY] * n + [VMEM] * 5 + [HBM] * len(held[1:]),
        out_specs=[HBM] * 3,
        out_shape=[whole] * 3,
        scratch_shapes=[
            pltpu.VMEM((1, PAIR, row_count, width), BF16),
            pltpu.VMEM((2, 3, block * PAIR, width), F32),
            pltpu.VMEM((3, row_count, PAIR, width), BF16),
            pltpu.SemaphoreType.DMA((1, n)),
            pltpu.SemaphoreType.DMA((3, block_count)),
        ],
        input_output_aliases={1 + n + 5 + i: i for i in range(len(held[1:]))},
        compiler_params=params(),
        cost_estimate=cost(10 * flops, 8 * PAIR * row_count * width),
    )(where, *g, *early[1:], *held[1:])
    return early[0], *late


def plan(per_group):
    last = per_group - 1
    first, second = range(per_group // 2), range(per_group // 2, last)
    units = []
    if first:
        units.append([(K, 0), (V, 0)])
        rest = [(a, c) for c in first for a in range(4)]
        units.append([x for x in rest if x not in units[0]])
    if second:
        units.append([(a, c) for c in second for a in range(4)])
    units += [[(K, last), (V, last), (Q, last)], [(G, last)]]
    return list(first), list(second), [sorted(u, key=lambda x: x[0] == G) for u in units]


def shards(queries, keys_in, values, cotangent):
    n = lax.axis_size("head")
    rows, head_count, width = queries.shape
    pair_count = head_count // PAIR
    per_group = pair_count // n
    last = per_group - 1
    where = jnp.stack([lax.axis_index("seq"), lax.axis_index("head")]).astype(jnp.int32)
    arrays = [
        x.reshape(rows, pair_count, PAIR, width) for x in (keys_in, values, queries, cotangent)
    ]
    first, second, units = plan(per_group)
    sent, arrived = [], []
    for i, items in enumerate(units):
        after = arrived[i - 2][1:] if i >= 2 else [s[0] for s in sent]
        sent.append(pack(where, arrays, items, n, after))
        arrived.append(exchange(sent[-1], n))
    ahead = own_rows_states(where, arrays, last, n, sent[1][:1])
    last_states = lax.all_gather(sum_to_group(ahead, n), "seq", axis=0)

    def place(a, chunk):
        u = next(u for u, items in enumerate(units) if (a, chunk) in items)
        return u, units[u].index((a, chunk))

    def batch_states(batch, after):
        sides = [place(a, c) + place(b, c) for c in batch for a, b in ((K, V), (Q, G))]
        used = sorted({u for s in sides for u in (s[0], s[2])})
        sides = [(used.index(u), a, used.index(w), b) for u, a, w, b in sides]
        own = shard_states([arrived[u] for u in used], sides, after)
        return own, lax.all_gather(own, "seq", axis=0)

    def compute(batch, states, chunk, outs, after):
        slots = [place(a, chunk) for a in range(4)]
        used = sorted({u for u, _ in slots})
        at = 2 * PAIR * batch.index(chunk)
        return compute_chunk(
            where,
            [arrived[u] for u in used],
            [(used.index(u), a) for u, a in slots],
            states[:, at : at + PAIR],
            states[:, at + PAIR : at + 2 * PAIR],
            outs,
            chunk,
            per_group,
            after,
        )

    outs = None
    after = []
    if first:
        _, first_states = batch_states(first, sent[min(3, len(sent) - 1)][:1])
        outs, token = compute(first, first_states, first[0], outs, [])
        after = [token]
    if second:
        own, second_states = batch_states(second, after)
        after = [own]
    for chunk in first[1:]:
        outs, token = compute(first, first_states, chunk, outs, after)
        after = [token]
    for chunk in second:
        outs, token = compute(second, second_states, chunk, outs, after)
        after = [token]
    results = last_chunk(
        where,
        arrived[-2],
        arrived[-1],
        last_states[:, :PAIR],
        last_states[:, PAIR:],
        outs,
        last,
        per_group,
        after,
    )
    return tuple(x.reshape(n * rows, per_group * PAIR, width) for x in results)


def solution(mesh):
    rows_spec = P(("seq", "head"), None, None)
    heads_spec = P("seq", "head", None)
    return jax.shard_map(
        shards, mesh=mesh, in_specs=(rows_spec,) * 4, out_specs=(heads_spec,) * 4, check_vma=False
    )
```

time: 297 us -> 273 us (0.919); the launches traced: 297 us -> 269 us
  starting transfers between devices: 63.3 us -> 36.3 us
  blocking collectives: 20 us -> 0 us
  local copies, waits for them, and re-layouts: 22.8 us -> 34.2 us
  waiting for transfers between devices: 107 us -> 116 us
    ppermute x27 -> x15, starting transfers between devices: 55 us -> 28.6 us  [exchange(): lax.ppermute(pieces[d], 'head', [(j, j ^ d) for j in range(n)])]
    all_gather x2 -> x0, blocking collectives: 20 us -> none  [the longest x1 10.1 us: shards(): lax.all_gather(shard_state(arrived['kv', last]), 'seq', axis=0)]
    pallas_call x5 -> x3, Pallas kernels: 42.3 us -> 25.8 us  [compute_chunk(): pl.pallas_call(functools.partial(chunk_kernel, n=n, block=block, chunk=ch...]
    pallas_call x14 -> x10, Pallas kernels: 26.7 us -> 41.1 us  [the longest x5 21.8 us: pack(): pl.pallas_call(functools.partial(pack_kernel, n=n, items=items), in_specs...]
    unnamed x146 -> x88, local copies, waits for them, and re-layouts: 18.6 us -> 27.6 us
    ppermute x3, waiting for transfers between devices: 2.17 us -> 8.52 us  [sum_to_group(): lax.ppermute(parts[d + bit], 'head', [(j, j ^ bit) for j in range(n)])]
    ppermute x27 -> x15, waiting for transfers between devices: 105 us -> 108 us  [exchange(): lax.ppermute(pieces[d], 'head', [(j, j ^ d) for j in range(n)])]
  transfers between devices with their start and end apart: 33 -> 21, of which waited for: 14 -> 9; matrix products, arithmetic and copies ran while one was open for 1% -> 3% of each run, Pallas kernels for 19% -> 19%
where the time goes in v1:
time: 273 us; the launch traced here: 269 us
  waiting for transfers between devices  116 us (42%)
  Pallas kernels  66.9 us (25%)
  starting transfers between devices  36.3 us (13%)
  local copies, waits for them, and re-layouts  34.2 us (13%)
  between operations  14.2 us (5%)
    ppermute x15, waiting for transfers between devices, exchange(): lax.ppermute(pieces[d], 'head', [(j, j ^ d) for j in range(n)])  108 us
    ppermute x15, starting transfers between devices, exchange(): lax.ppermute(pieces[d], 'head', [(j, j ^ d) for j in range(n)])  28.6 us
    unnamed x88, local copies, waits for them, and re-layouts  27.6 us
    pallas_call x3, Pallas kernels, compute_chunk(): pl.pallas_call(functools.partial(chunk_kernel, n=n, block=block, chunk=ch...  25.8 us
    pallas_call x5, Pallas kernels, pack(): pl.pallas_call(functools.partial(pack_kernel, n=n, items=items), in_specs...  21.8 us
    ppermute x3, waiting for transfers between devices, sum_to_group(): lax.ppermute(parts[d + bit], 'head', [(j, j ^ bit) for j in range(n)])  8.52 us
    ppermute x3, starting transfers between devices, sum_to_group(): lax.ppermute(parts[d + bit], 'head', [(j, j ^ bit) for j in range(n)])  7.65 us
    pallas_call x1, Pallas kernels, last_chunk(): pl.pallas_call(functools.partial(late_kernel, n=n, block=block, chunk=chu...  5.5 us
  transfers between devices with their start and end apart: 21, of which 9 were waited for; matrix products, arithmetic and copies ran while one was open for 3% of the time, Pallas kernels for 19%

profile of v1, /device:TPU:0, one launch (start us, length us, event | category | flops | bytes accessed | tf_op | source)
XLA Modules:
  0.0 268.6 jit_solution(10618308923517193331)
XLA Ops:
  7.2 0.1 pad_add_fusion.where
  7.3 1.6 copy-done
  8.9 1.6 copy-done.2
  10.5 1.6 copy-done.6
  12.1 1.6 copy-done.10
  13.7 2.4 shard_map.75
  16.0 6.1 %shard_map.76 = (bf16[6,2,256,128]{3,2,1,0:T(8,128)(2,1)S(1)}, bf16[6,2,256,128]{3,2,1,0:T(8,128)(2,1)S(1)}, bf16[6,2,256,128]{3,2,1,0:T(8,128)(2,1)S(1)}, bf16[6,2,256,128]{3,2,1,0:T(8,128)(2,1)S(1)}) custom-call(s32[2]{0:T(128)S(1)} %pad_add_fusion.where, bf16[256,16,2,128]{3,2,1,0:T(2,128)(2,1)S(1)} %bitcast.14, bf16[256,16,2,128]{3,2,1,0:T(2,128)(2,1)S(1)} %bitcast.20, ...), custom_call_target="tpu_custom_call" | custom-call | bytes 6291456 | tf_op jit(solution)/shard_map/pallas_call | solution.py:107
  22.1 3.1 %collective-permute-start = (bf16[6,2,256,128]{3,2,1,0:T(8,128)(2,1)S(1)}, bf16[6,2,256,128]{3,2,1,0:T(8,128)(2,1)S(1)}, u32[]{:S(2)}, u32[]{:S(2)}) collective-permute-start(bf16[6,2,256,128]{3,2,1,0:T(8,128)(2,1)S(1)} %get-tuple-element.53), channel_id=1, source_target_pairs={{0,1},{1,0},{2,3},{3,2},{4,5},{5,4},{6,7},{7,6},{8,9},{9,8},{10,11... | collective-permute-start | bytes 2359304 | tf_op jit(solution)/shard_map/ppermute | solution.py:127
  25.2 2.6 collective-permute-start.1
  27.8 1.9 collective-permute-start.10
  29.7 1.9 collective-permute-start.11
  31.6 27.2 %collective-permute-done.refs_4_.refs_5_.refs_1_ = bf16[6,2,256,128]{3,2,1,0:T(8,128)(2,1)S(1)} collective-permute-done((bf16[6,2,256,128]{3,2,1,0:T(8,128)(2,1)S(1)}, bf16[6,2,256,128]{3,2,1,0:T(8,128)(2,1)S(1)}, u32[]{:S(2)}, u32[]{:S(2)}) %collective-permute-start) | collective-permute-done | bytes 786464 | tf_op jit(solution)/shard_map/ppermute | solution.py:127
  58.9 32.7 %collective-permute-done.1.refs_5_.refs_6_.refs_2_ = bf16[6,2,256,128]{3,2,1,0:T(8,128)(2,1)S(1)} collective-permute-done((bf16[6,2,256,128]{3,2,1,0:T(8,128)(2,1)S(1)}, bf16[6,2,256,128]{3,2,1,0:T(8,128)(2,1)S(1)}, u32[]{:S(2)}, u32[]{:S(2)}) %collective-permute-start.1) | collective-permute-done | bytes 786464 | tf_op jit(solution)/shard_map/ppermute | solution.py:127
  91.6 4.9 %shard_map.77 = (bf16[3,2,256,128]{3,2,1,0:T(8,128)(2,1)S(1)}, bf16[3,2,256,128]{3,2,1,0:T(8,128)(2,1)}, bf16[3,2,256,128]{3,2,1,0:T(8,128)(2,1)}, bf16[3,2,256,128]{3,2,1,0:T(8,128)(2,1)}) custom-call(s32[2]{0:T(128)S(1)} %pad_add_fusion.where, bf16[256,16,2,128]{3,2,1,0:T(2,128)(2,1)S(1)} %bitcast.15, bf16[256,16,2,128]{3,2,1,0:T(2,128)(2,1)S(1)} %bitcast.21, ...), custom_call_target="tpu_custom_call" | custom-call | bytes 3145728 | tf_op jit(solution)/shard_map/pallas_call | solution.py:107
  96.5 17.5 %collective-permute-done.10.refs_5_.refs_2_ = bf16[2,2,256,128]{3,2,1,0:T(8,128)(2,1)S(1)} collective-permute-done((bf16[2,2,256,128]{3,2,1,0:T(8,128)(2,1)S(1)}, bf16[2,2,256,128]{3,2,1,0:T(8,128)(2,1)S(1)}, u32[]{:S(2)}, u32[]{:S(2)}) %collective-permute-start.10) | collective-permute-done | bytes 262176 | tf_op jit(solution)/shard_map/ppermute | solution.py:127
  114.1 1.0 shard_map.80
  115.1 0.7 copy-done.29
  115.8 0.8 copy-done.39
  116.6 0.7 copy-done.41
  117.4 1.6 copy-done.3
  118.9 1.6 copy-done.7
  120.5 1.6 copy-done.11
  122.1 5.0 %shard_map.78 = (bf16[4,128,128]{2,1,0:T(8,128)(2,1)S(1)}, bf16[4,128,128]{2,1,0:T(8,128)(2,1)S(1)}, bf16[4,128,128]{2,1,0:T(8,128)(2,1)S(1)}, bf16[4,128,128]{2,1,0:T(8,128)(2,1)S(1)}) custom-call(s32[2]{0:T(128)S(1)} %pad_add_fusion.where, bf16[256,16,2,128]{3,2,1,0:T(2,128)(2,1)S(1)} %bitcast.16, bf16[256,16,2,128]{3,2,1,0:T(2,128)(2,1)S(1)} %bitcast.22, ...), custom_call_target="tpu_custom_call" | custom-call | flops 134217728 | bytes 4194304 | tf_op jit(solution)/shard_map/pallas_call | solution.py:153
  127.1 4.8 %collective-permute-start.7 = (bf16[4,128,128]{2,1,0:T(8,128)(2,1)S(1)}, bf16[4,128,128]{2,1,0:T(8,128)(2,1)S(1)}, u32[]{:S(2)}, u32[]{:S(2)}) collective-permute-start(bf16[4,128,128]{2,1,0:T(8,128)(2,1)S(1)} %get-tuple-element.64), channel_id=1, source_target_pairs={{0,1},{1,0},{2,3},{3,2},{4,5},{5,4},{6,7},{7,6},{8,9},{9,8},{10,11... | collective-permute-start | bytes 393224 | tf_op jit(solution)/shard_map/ppermute | solution.py:174
  131.9 0.1 collective-permute-start.6
  132.0 3.7 %collective-permute-done.7 = bf16[4,128,128]{2,1,0:T(8,128)(2,1)S(1)} collective-permute-done((bf16[4,128,128]{2,1,0:T(8,128)(2,1)S(1)}, bf16[4,128,128]{2,1,0:T(8,128)(2,1)S(1)}, u32[]{:S(2)}, u32[]{:S(2)}) %collective-permute-start.7) | collective-permute-done | bytes 131104 | tf_op jit(solution)/shard_map/ppermute | solution.py:174
  135.8 2.8 %collective-permute-start.8 = (bf16[4,128,128]{2,1,0:T(8,128)(2,1)S(1)}, bf16[4,128,128]{2,1,0:T(8,128)(2,1)S(1)}, u32[]{:S(2)}, u32[]{:S(2)}) collective-permute-start(bf16[4,128,128]{2,1,0:T(8,128)(2,1)S(1)} %add_convert_fusion.1), channel_id=1, source_target_pairs={{0,2},{1,3},{2,0},{3,1},{4,6},{5,7},{6,4},{7,5},{8,10},{9,11},{10,... | collective-permute-start | bytes 393224 | tf_op jit(solution)/shard_map/ppermute | solution.py:174
  138.6 4.8 %collective-permute-done.8 = bf16[4,128,128]{2,1,0:T(8,128)(2,1)S(1)} collective-permute-done((bf16[4,128,128]{2,1,0:T(8,128)(2,1)S(1)}, bf16[4,128,128]{2,1,0:T(8,128)(2,1)S(1)}, u32[]{:S(2)}, u32[]{:S(2)}) %collective-permute-start.8) | collective-permute-done | bytes 131104 | tf_op jit(solution)/shard_map/ppermute | solution.py:174
  143.4 0.7 add_convert_fusion
  144.2 1.6 copy-done.4
  145.8 1.6 copy-done.8
  147.4 1.6 copy-done.12
  149.0 0.9 copy-done.30
  149.9 5.5 %shard_map.79 = (bf16[4,2,256,128]{3,2,1,0:T(8,128)(2,1)S(1)}, bf16[4,2,256,128]{3,2,1,0:T(8,128)(2,1)}, bf16[4,2,256,128]{3,2,1,0:T(8,128)(2,1)}, bf16[4,2,256,128]{3,2,1,0:T(8,128)(2,1)}) custom-call(s32[2]{0:T(128)S(1)} %pad_add_fusion.where, bf16[256,16,2,128]{3,2,1,0:T(2,128)(2,1)S(1)} %bitcast.17, bf16[256,16,2,128]{3,2,1,0:T(2,128)(2,1)S(1)} %bitcast.23, ...), custom_call_target="tpu_custom_call" | custom-call | bytes 4194304 | tf_op jit(solution)/shard_map/pallas_call | solution.py:107
  155.5 0.8 copy-done.36
  156.3 0.2 collective-permute-start.12
  156.5 2.7 %collective-permute-start.13 = (bf16[4,2,256,128]{3,2,1,0:T(8,128)(2,1)}, bf16[4,2,256,128]{3,2,1,0:T(8,128)(2,1)}, u32[]{:S(2)}, u32[]{:S(2)}) collective-permute-start(bf16[4,2,256,128]{3,2,1,0:T(8,128)(2,1)} %get-tuple-element.70), channel_id=1, source_target_pairs={{0,2},{1,3},{2,0},{3,1},{4,6},{5,7},{6,4},{7,5},{8,10},{9,11},{10,... | collective-permute-start | bytes 1572872 | tf_op jit(solution)/shard_map/ppermute | solution.py:127
  159.2 1.5 collective-permute-start.14
  160.7 3.0 %fusion = (bf16[8,2,128,128]{3,2,1,0:T(8,128)(2,1)}, bf16[8,2,128,128]{3,2,1,0:T(8,128)(2,1)}, bf16[8,2,128,128]{3,2,1,0:T(8,128)(2,1)S(1)}, bf16[8,2,128,128]{3,2,1,0:T(8,128)(2,1)S(1)}) fusion(bf16[8,8,128,128]{3,2,1,0:T(8,128)(2,1)} %bitcast.41), kind=kLoop, calls=%fused_computation.4 | loop fusion | bytes 4194304 | tf_op jit(solution)/shard_map/slice | solution.py:519
  163.7 8.6 %shard_map.81 = (bf16[1024,4,2,128]{3,2,1,0:T(2,128)(2,1)}, bf16[1024,4,2,128]{3,2,1,0:T(2,128)(2,1)}, bf16[1024,4,2,128]{3,2,1,0:T(2,128)(2,1)}, bf16[1024,4,2,128]{3,2,1,0:T(2,128)(2,1)}, f32[8,128]{1,0:T(8,128)S(1)}) custom-call(s32[2]{0:T(128)S(1)} %pad_add_fusion.where, bf16[2,2,256,128]{3,2,1,0:T(8,128)(2,1)S(1)} %copy-done.24, ...), custom_call_target="tpu_custom_call" | custom-call | flops 1409286144 | bytes 4194304 | tf_op jit(solution)/shard_map/pallas_call | solution.py:322
  172.4 3.7 %collective-permute-done.12.refs_1_.refs_4_ = bf16[4,2,256,128]{3,2,1,0:T(8,128)(2,1)S(1)} collective-permute-done((bf16[4,2,256,128]{3,2,1,0:T(8,128)(2,1)}, bf16[4,2,256,128]{3,2,1,0:T(8,128)(2,1)S(1)}, u32[]{:S(2)}, u32[]{:S(2)}) %collective-permute-start.12) | collective-permute-done | bytes 524320 | tf_op jit(solution)/shard_map/ppermute | solution.py:127
  176.0 19.0 %collective-permute-done.13.refs_2_.refs_5_ = bf16[4,2,256,128]{3,2,1,0:T(8,128)(2,1)} collective-permute-done((bf16[4,2,256,128]{3,2,1,0:T(8,128)(2,1)}, bf16[4,2,256,128]{3,2,1,0:T(8,128)(2,1)}, u32[]{:S(2)}, u32[]{:S(2)}) %collective-permute-start.13) | collective-permute-done | bytes 524320 | tf_op jit(solution)/shard_map/ppermute | solution.py:127
  195.0 2.5 shard_map.82.refs_10_
  197.6 1.6 copy-done.5
  199.2 1.6 copy-done.9
  200.8 1.6 copy-done.13
  202.3 2.9 %shard_map.86 = (bf16[1,2,256,128]{3,2,1,0:T(8,128)(2,1)S(1)}, bf16[1,2,256,128]{3,2,1,0:T(8,128)(2,1)}, bf16[1,2,256,128]{3,2,1,0:T(8,128)(2,1)}, bf16[1,2,256,128]{3,2,1,0:T(8,128)(2,1)S(1)}) custom-call(s32[2]{0:T(128)S(1)} %pad_add_fusion.where, bf16[256,16,2,128]{3,2,1,0:T(2,128)(2,1)S(1)} %bitcast.18, bf16[256,16,2,128]{3,2,1,0:T(2,128)(2,1)S(1)} %bitcast.24, ...), custom_call_target="tpu_custom_call" | custom-call | bytes 1048576 | tf_op jit(solution)/shard_map/pallas_call | solution.py:107
  205.3 0.7 copy-done.42
  205.9 8.2 %collective-permute-start.15 = (bf16[1,2,256,128]{3,2,1,0:T(8,128)(2,1)}, bf16[1,2,256,128]{3,2,1,0:T(8,128)(2,1)}, u32[]{:S(2)}, u32[]{:S(2)}) collective-permute-start(bf16[1,2,256,128]{3,2,1,0:T(8,128)(2,1)} %get-tuple-element.86), channel_id=1, source_target_pairs={{0,1},{1,0},{2,3},{3,2},{4,5},{5,4},{6,7},{7,6},{8,9},{9,8},{10,11... | collective-permute-start | bytes 393224 | tf_op jit(solution)/shard_map/ppermute | solution.py:127
  214.1 0.1 collective-permute-start.16
  214.1 2.0 collective-permute-start.3
  216.1 1.0 collective-permute-start.4
  217.1 1.5 collective-permute-start.5
  218.5 2.3 fusion.2
  220.9 1.1 copy-done.22
  222.0 1.0 copy-done.33
  223.0 8.6 %shard_map.83 = (bf16[1024,4,2,128]{3,2,1,0:T(2,128)(2,1)}, bf16[1024,4,2,128]{3,2,1,0:T(2,128)(2,1)}, bf16[1024,4,2,128]{3,2,1,0:T(2,128)(2,1)}, bf16[1024,4,2,128]{3,2,1,0:T(2,128)(2,1)}, f32[8,128]{1,0:T(8,128)S(1)}) custom-call(s32[2]{0:T(128)S(1)} %pad_add_fusion.where, ...), custom_call_target="tpu_custom_call", output_to_operand_aliasing={{0}: (7, {}), {1}: (8, {}), {2}: (9, {}), {3}: (10, {})} | custom-call | flops 1409286144 | bytes 4194304 | tf_op jit(solution)/shard_map/pallas_call | solution.py:322
  231.7 1.4 fusion.1
  233.0 0.4 collective-permute-done.3.refs_1_
  233.5 2.0 collective-permute-start.17
  235.5 8.7 %shard_map.84 = (bf16[1024,4,2,128]{3,2,1,0:T(2,128)(2,1)}, bf16[1024,4,2,128]{3,2,1,0:T(2,128)(2,1)}, bf16[1024,4,2,128]{3,2,1,0:T(2,128)(2,1)}, bf16[1024,4,2,128]{3,2,1,0:T(2,128)(2,1)}, f32[8,128]{1,0:T(8,128)S(1)}) custom-call(s32[2]{0:T(128)S(1)} %pad_add_fusion.where, ...), custom_call_target="tpu_custom_call", output_to_operand_aliasing={{0}: (7, {}), {1}: (8, {}), {2}: (9, {}), {3}: (10, {})} | custom-call | flops 1409286144 | bytes 4194304 | tf_op jit(solution)/shard_map/pallas_call | solution.py:322
  244.2 7.0 %collective-permute-done.4.refs_2_ = bf16[3,2,256,128]{3,2,1,0:T(8,128)(2,1)} collective-permute-done((bf16[3,2,256,128]{3,2,1,0:T(8,128)(2,1)}, bf16[3,2,256,128]{3,2,1,0:T(8,128)(2,1)}, u32[]{:S(2)}, u32[]{:S(2)}) %collective-permute-start.4) | collective-permute-done | bytes 393248 | tf_op jit(solution)/shard_map/ppermute | solution.py:127
  251.2 5.3 %shard_map.85 = (bf16[1024,4,2,128]{3,2,1,0:T(2,128)(2,1)}, bf16[3,2,1024,128]{3,2,1,0:T(8,128)(2,1)S(1)}, bf16[4,2,256,256]{3,2,1,0:T(8,128)(2,1)S(1)}, bf16[4,...) custom-call(s32[2]{0:T(128)S(1)} %pad_add_fusion.where, ...), custom_call_target="tpu_custom_call", output_to_operand_aliasing={{0}: (7, {})} | custom-call | flops 603979776 | bytes 2097152 | tf_op jit(solution)/shard_map/pallas_call | solution.py:432
  256.5 5.5 %shard_map.87 = (bf16[1024,4,2,128]{3,2,1,0:T(2,128)(2,1)}, bf16[1024,4,2,128]{3,2,1,0:T(2,128)(2,1)}, bf16[1024,4,2,128]{3,2,1,0:T(2,128)(2,1)}) custom-call(s32[2]{0:T(128)S(1)} %pad_add_fusion.where, bf16[1,2,256,128]{3,2,1,0:T(8,128)(2,1)S(1)} %get-tuple-element.85.refs_0_, ...), custom_call_target="tpu_custom_call", output_to_operand_aliasing={{0}: (10, {}), {1}: (11, {}), {2}: (12, {})} | custom-call | flops 1006632960 | bytes 2097152 | tf_op jit(solution)/shard_map/pallas_call | solution.py:447
  (88 shorter events, 0.4 us)
Async XLA Ops:
  7.2 153.5 %all-gather.9.cloned.1.call-start = ((), (), s32[]{:S(2)}) async-start(), calls=%async_computation.1 | async-start | bytes 2359296 | tf_op jit(solution)/shard_map/all_gather | solution.py:508
  7.3 1.6 copy-start
  8.9 1.6 copy-start.2
  10.5 1.6 copy-start.6
  12.1 1.6 copy-start.10
  16.0 98.0 %copy-start.23 = (bf16[2,2,256,128]{3,2,1,0:T(8,128)(2,1)}, bf16[2,2,256,128]{3,2,1,0:T(8,128)(2,1)S(1)}, u32[]{:S(2)}) copy-start(bf16[2,2,256,128]{3,2,1,0:T(8,128)(2,1)S(1)} %get-tuple-element.52.refs_4_.refs_0_) | copy-start | bytes 786436
  22.1 36.7 %collective-permute-start = (bf16[6,2,256,128]{3,2,1,0:T(8,128)(2,1)S(1)}, bf16[6,2,256,128]{3,2,1,0:T(8,128)(2,1)S(1)}, u32[]{:S(2)}, u32[]{:S(2)}) collective-permute-start(bf16[6,2,256,128]{3,2,1,0:T(8,128)(2,1)S(1)} %get-tuple-element.53), channel_id=1, source_target_pairs={{0,1},{1,0},{2,3},{3,2},{4,5},{5,4},{6,7},{7,6},{8,9},{9,8},{10,11... | collective-permute-start | bytes 2359304 | tf_op jit(solution)/shard_map/ppermute | solution.py:127
  25.2 66.4 %collective-permute-start.1 = (bf16[6,2,256,128]{3,2,1,0:T(8,128)(2,1)S(1)}, bf16[6,2,256,128]{3,2,1,0:T(8,128)(2,1)S(1)}, u32[]{:S(2)}, u32[]{:S(2)}) collective-permute-start(bf16[6,2,256,128]{3,2,1,0:T(8,128)(2,1)S(1)} %get-tuple-element.54), channel_id=1, source_target_pairs={{0,2},{1,3},{2,0},{3,1},{4,6},{5,7},{6,4},{7,5},{8,10},{9,11},{10,... | collective-permute-start | bytes 2359304 | tf_op jit(solution)/shard_map/ppermute | solution.py:127
  27.8 63.8 %collective-permute-start.2 = (bf16[6,2,256,128]{3,2,1,0:T(8,128)(2,1)S(1)}, bf16[6,2,256,128]{3,2,1,0:T(8,128)(2,1)S(1)}, u32[]{:S(2)}, u32[]{:S(2)}) collective-permute-start(bf16[6,2,256,128]{3,2,1,0:T(8,128)(2,1)S(1)} %get-tuple-element.55), channel_id=1, source_target_pairs={{0,3},{1,2},{2,1},{3,0},{4,7},{5,6},{6,5},{7,4},{8,11},{9,10},{10,... | collective-permute-start | bytes 2359304 | tf_op jit(solution)/shard_map/ppermute | solution.py:127
  27.8 86.2 %collective-permute-start.10 = (bf16[2,2,256,128]{3,2,1,0:T(8,128)(2,1)S(1)}, bf16[2,2,256,128]{3,2,1,0:T(8,128)(2,1)S(1)}, u32[]{:S(2)}, u32[]{:S(2)}) collective-permute-start(bf16[2,2,256,128]{3,2,1,0:T(8,128)(2,1)S(1)} %get-tuple-element.66), channel_id=1, source_target_pairs={{0,2},{1,3},{2,0},{3,1},{4,6},{5,7},{6,4},{7,5},{8,10},{9,11},{10,... | collective-permute-start | bytes 786440 | tf_op jit(solution)/shard_map/ppermute | solution.py:127
  29.7 84.3 %collective-permute-start.11 = (bf16[2,2,256,128]{3,2,1,0:T(8,128)(2,1)S(1)}, bf16[2,2,256,128]{3,2,1,0:T(8,128)(2,1)S(1)}, u32[]{:S(2)}, u32[]{:S(2)}) collective-permute-start(bf16[2,2,256,128]{3,2,1,0:T(8,128)(2,1)S(1)} %get-tuple-element.67), channel_id=1, source_target_pairs={{0,3},{1,2},{2,1},{3,0},{4,7},{5,6},{6,5},{7,4},{8,11},{9,10},{10,... | collective-permute-start | bytes 786440 | tf_op jit(solution)/shard_map/ppermute | solution.py:127
  58.9 55.2 %copy-start.14 = (bf16[6,2,256,128]{3,2,1,0:T(8,128)(2,1)}, bf16[6,2,256,128]{3,2,1,0:T(8,128)(2,1)S(1)}, u32[]{:S(2)}) copy-start(bf16[6,2,256,128]{3,2,1,0:T(8,128)(2,1)S(1)} %collective-permute-done.refs_4_.refs_5_.refs_1_) | copy-start | bytes 2359300
  58.9 55.2 %collective-permute-start.9 = (bf16[2,2,256,128]{3,2,1,0:T(8,128)(2,1)S(1)}, bf16[2,2,256,128]{3,2,1,0:T(8,128)(2,1)S(1)}, u32[]{:S(2)}, u32[]{:S(2)}) collective-permute-start(bf16[2,2,256,128]{3,2,1,0:T(8,128)(2,1)S(1)} %get-tuple-element.65), channel_id=1, source_target_pairs={{0,1},{1,0},{2,3},{3,2},{4,5},{5,4},{6,7},{7,6},{8,9},{9,8},{10,11... | collective-permute-start | bytes 786440 | tf_op jit(solution)/shard_map/ppermute | solution.py:127
  91.6 22.5 %copy-start.17 = (bf16[6,2,256,128]{3,2,1,0:T(8,128)(2,1)}, bf16[6,2,256,128]{3,2,1,0:T(8,128)(2,1)S(1)}, u32[]{:S(2)}) copy-start(bf16[6,2,256,128]{3,2,1,0:T(8,128)(2,1)S(1)} %collective-permute-done.1.refs_5_.refs_6_.refs_2_) | copy-start | bytes 2359300
  91.6 22.5 %copy-start.20 = (bf16[6,2,256,128]{3,2,1,0:T(8,128)(2,1)}, bf16[6,2,256,128]{3,2,1,0:T(8,128)(2,1)S(1)}, u32[]{:S(2)}) copy-start(bf16[6,2,256,128]{3,2,1,0:T(8,128)(2,1)S(1)} %collective-permute-done.2.refs_6_.refs_7_.refs_3_) | copy-start | bytes 2359300
  114.1 30.1 %copy-start.25 = (bf16[2,2,256,128]{3,2,1,0:T(8,128)(2,1)}, bf16[2,2,256,128]{3,2,1,0:T(8,128)(2,1)S(1)}, u32[]{:S(2)}) copy-start(bf16[2,2,256,128]{3,2,1,0:T(8,128)(2,1)S(1)} %collective-permute-done.10.refs_5_.refs_2_) | copy-start | bytes 786436
  114.1 30.1 %copy-start.27 = (bf16[2,2,256,128]{3,2,1,0:T(8,128)(2,1)}, bf16[2,2,256,128]{3,2,1,0:T(8,128)(2,1)S(1)}, u32[]{:S(2)}) copy-start(bf16[2,2,256,128]{3,2,1,0:T(8,128)(2,1)S(1)} %collective-permute-done.11.refs_6_.refs_3_) | copy-start | bytes 786436
  114.1 3.2 %copy-start.1 = (bf16[256,32,128]{2,1,0:T(8,128)(2,1)S(1)}, bf16[256,32,128]{2,1,0:T(8,128)(2,1)}, u32[]{:S(2)}) copy-start(bf16[256,32,128]{2,1,0:T(8,128)(2,1)} %param.5) | copy-start | bytes 6291460
  115.1 0.7 copy-start.29
  115.8 0.8 copy-start.39
  116.5 0.7 copy-start.41
  117.3 101.3 %all-gather.7.cloned.1.call-start = ((), (), s32[]{:S(2)}) async-start(), calls=%async_computation | async-start | bytes 1179648 | tf_op jit(solution)/shard_map/all_gather | solution.py:497
  117.4 1.6 copy-start.3
  118.9 1.6 copy-start.7
  120.5 1.6 copy-start.11
  127.1 8.6 %collective-permute-start.7 = (bf16[4,128,128]{2,1,0:T(8,128)(2,1)S(1)}, bf16[4,128,128]{2,1,0:T(8,128)(2,1)S(1)}, u32[]{:S(2)}, u32[]{:S(2)}) collective-permute-start(bf16[4,128,128]{2,1,0:T(8,128)(2,1)S(1)} %get-tuple-element.64), channel_id=1, source_target_pairs={{0,1},{1,0},{2,3},{3,2},{4,5},{5,4},{6,7},{7,6},{8,9},{9,8},{10,11... | collective-permute-start | bytes 393224 | tf_op jit(solution)/shard_map/ppermute | solution.py:174
  131.9 6.6 %collective-permute-start.6 = (bf16[4,128,128]{2,1,0:T(8,128)(2,1)S(1)}, bf16[4,128,128]{2,1,0:T(8,128)(2,1)S(1)}, u32[]{:S(2)}, u32[]{:S(2)}) collective-permute-start(bf16[4,128,128]{2,1,0:T(8,128)(2,1)S(1)} %get-tuple-element.62), channel_id=1, source_target_pairs={{0,1},{1,0},{2,3},{3,2},{4,5},{5,4},{6,7},{7,6},{8,9},{9,8},{10,11... | collective-permute-start | bytes 393224 | tf_op jit(solution)/shard_map/ppermute | solution.py:174
  135.8 7.6 %collective-permute-start.8 = (bf16[4,128,128]{2,1,0:T(8,128)(2,1)S(1)}, bf16[4,128,128]{2,1,0:T(8,128)(2,1)S(1)}, u32[]{:S(2)}, u32[]{:S(2)}) collective-permute-start(bf16[4,128,128]{2,1,0:T(8,128)(2,1)S(1)} %add_convert_fusion.1), channel_id=1, source_target_pairs={{0,2},{1,3},{2,0},{3,1},{4,6},{5,7},{6,4},{7,5},{8,10},{9,11},{10,... | collective-permute-start | bytes 393224 | tf_op jit(solution)/shard_map/ppermute | solution.py:174
  144.1 87.6 %all-gather.11.cloned.1.call-start = ((), (), s32[]{:S(2)}) async-start(), calls=%async_computation.2 | async-start | bytes 1179648 | tf_op jit(solution)/shard_map/all_gather | solution.py:508
  144.2 1.6 copy-start.4
  145.8 1.6 copy-start.8
  147.4 1.6 copy-start.12
  149.0 0.9 copy-start.30
  155.5 0.8 copy-start.36
  156.3 19.7 %collective-permute-start.12 = (bf16[4,2,256,128]{3,2,1,0:T(8,128)(2,1)}, bf16[4,2,256,128]{3,2,1,0:T(8,128)(2,1)S(1)}, u32[]{:S(2)}, u32[]{:S(2)}) collective-permute-start(bf16[4,2,256,128]{3,2,1,0:T(8,128)(2,1)} %get-tuple-element.69), channel_id=1, source_target_pairs={{0,1},{1,0},{2,3},{3,2},{4,5},{5,4},{6,7},{7,6},{8,9},{9,8},{10,11... | collective-permute-start | bytes 1572872 | tf_op jit(solution)/shard_map/ppermute | solution.py:127
  156.5 38.5 %collective-permute-start.13 = (bf16[4,2,256,128]{3,2,1,0:T(8,128)(2,1)}, bf16[4,2,256,128]{3,2,1,0:T(8,128)(2,1)}, u32[]{:S(2)}, u32[]{:S(2)}) collective-permute-start(bf16[4,2,256,128]{3,2,1,0:T(8,128)(2,1)} %get-tuple-element.70), channel_id=1, source_target_pairs={{0,2},{1,3},{2,0},{3,1},{4,6},{5,7},{6,4},{7,5},{8,10},{9,11},{10,... | collective-permute-start | bytes 1572872 | tf_op jit(solution)/shard_map/ppermute | solution.py:127
  159.2 35.9 %collective-permute-start.14 = (bf16[4,2,256,128]{3,2,1,0:T(8,128)(2,1)}, bf16[4,2,256,128]{3,2,1,0:T(8,128)(2,1)}, u32[]{:S(2)}, u32[]{:S(2)}) collective-permute-start(bf16[4,2,256,128]{3,2,1,0:T(8,128)(2,1)} %get-tuple-element.71), channel_id=1, source_target_pairs={{0,3},{1,2},{2,1},{3,0},{4,7},{5,6},{6,5},{7,4},{8,11},{9,10},{10,... | collective-permute-start | bytes 1572872 | tf_op jit(solution)/shard_map/ppermute | solution.py:127
  160.7 3.0 %copy-start.15 = (bf16[6,2,256,128]{3,2,1,0:T(8,128)(2,1)S(1)}, bf16[6,2,256,128]{3,2,1,0:T(8,128)(2,1)}, u32[]{:S(2)}) copy-start(bf16[6,2,256,128]{3,2,1,0:T(8,128)(2,1)} %copy-done.14) | copy-start | bytes 2359300
  160.7 3.0 %copy-start.18 = (bf16[6,2,256,128]{3,2,1,0:T(8,128)(2,1)S(1)}, bf16[6,2,256,128]{3,2,1,0:T(8,128)(2,1)}, u32[]{:S(2)}) copy-start(bf16[6,2,256,128]{3,2,1,0:T(8,128)(2,1)} %copy-done.17) | copy-start | bytes 2359300
  160.7 3.0 %copy-start.21 = (bf16[6,2,256,128]{3,2,1,0:T(8,128)(2,1)S(1)}, bf16[6,2,256,128]{3,2,1,0:T(8,128)(2,1)}, u32[]{:S(2)}) copy-start(bf16[6,2,256,128]{3,2,1,0:T(8,128)(2,1)} %copy-done.20) | copy-start | bytes 2359300
  160.7 3.0 %copy-start.24 = (bf16[2,2,256,128]{3,2,1,0:T(8,128)(2,1)S(1)}, bf16[2,2,256,128]{3,2,1,0:T(8,128)(2,1)}, u32[]{:S(2)}) copy-start(bf16[2,2,256,128]{3,2,1,0:T(8,128)(2,1)} %copy-done.23) | copy-start | bytes 786436
  160.7 3.0 %copy-start.26 = (bf16[2,2,256,128]{3,2,1,0:T(8,128)(2,1)S(1)}, bf16[2,2,256,128]{3,2,1,0:T(8,128)(2,1)}, u32[]{:S(2)}) copy-start(bf16[2,2,256,128]{3,2,1,0:T(8,128)(2,1)} %copy-done.25) | copy-start | bytes 786436
  160.7 3.0 %copy-start.28 = (bf16[2,2,256,128]{3,2,1,0:T(8,128)(2,1)S(1)}, bf16[2,2,256,128]{3,2,1,0:T(8,128)(2,1)}, u32[]{:S(2)}) copy-start(bf16[2,2,256,128]{3,2,1,0:T(8,128)(2,1)} %copy-done.27) | copy-start | bytes 786436
  160.7 3.0 %copy-start.31 = (bf16[2,2,256,128]{3,2,1,0:T(8,128)(2,1)S(1)}, bf16[2,2,256,128]{3,2,1,0:T(8,128)(2,1)}, u32[]{:S(2)}) copy-start(bf16[2,2,256,128]{3,2,1,0:T(8,128)(2,1)} %copy-done.29) | copy-start | bytes 786436
  163.7 31.3 %copy-start.37 = (bf16[4,2,256,128]{3,2,1,0:T(8,128)(2,1)S(1)}, bf16[4,2,256,128]{3,2,1,0:T(8,128)(2,1)}, u32[]{:S(2)}) copy-start(bf16[4,2,256,128]{3,2,1,0:T(8,128)(2,1)} %copy-done.36) | copy-start | bytes 1572868
  197.6 1.6 copy-start.5
  199.2 1.6 copy-start.9
  200.8 1.6 copy-start.13
  205.9 14.9 %copy-start.16 = (bf16[6,2,256,128]{3,2,1,0:T(8,128)(2,1)S(1)}, bf16[6,2,256,128]{3,2,1,0:T(8,128)(2,1)}, u32[]{:S(2)}) copy-start(bf16[6,2,256,128]{3,2,1,0:T(8,128)(2,1)} %copy-done.14) | copy-start | bytes 2359300
  205.9 14.9 %copy-start.19 = (bf16[6,2,256,128]{3,2,1,0:T(8,128)(2,1)S(1)}, bf16[6,2,256,128]{3,2,1,0:T(8,128)(2,1)}, u32[]{:S(2)}) copy-start(bf16[6,2,256,128]{3,2,1,0:T(8,128)(2,1)} %copy-done.17) | copy-start | bytes 2359300
  205.9 14.9 %copy-start.32 = (bf16[8,2,128,128]{3,2,1,0:T(8,128)(2,1)S(1)}, bf16[8,2,128,128]{3,2,1,0:T(8,128)(2,1)}, u32[]{:S(2)}) copy-start(bf16[8,2,128,128]{3,2,1,0:T(8,128)(2,1)} %get-tuple-element.100.refs_5_) | copy-start | bytes 1572868
  205.9 50.6 %collective-permute-start.15 = (bf16[1,2,256,128]{3,2,1,0:T(8,128)(2,1)}, bf16[1,2,256,128]{3,2,1,0:T(8,128)(2,1)}, u32[]{:S(2)}, u32[]{:S(2)}) collective-permute-start(bf16[1,2,256,128]{3,2,1,0:T(8,128)(2,1)} %get-tuple-element.86), channel_id=1, source_target_pairs={{0,1},{1,0},{2,3},{3,2},{4,5},{5,4},{6,7},{7,6},{8,9},{9,8},{10,11... | collective-permute-start | bytes 393224 | tf_op jit(solution)/shard_map/ppermute | solution.py:127
  214.1 42.4 %collective-permute-start.16 = (bf16[1,2,256,128]{3,2,1,0:T(8,128)(2,1)}, bf16[1,2,256,128]{3,2,1,0:T(8,128)(2,1)}, u32[]{:S(2)}, u32[]{:S(2)}) collective-permute-start(bf16[1,2,256,128]{3,2,1,0:T(8,128)(2,1)} %get-tuple-element.87), channel_id=1, source_target_pairs={{0,2},{1,3},{2,0},{3,1},{4,6},{5,7},{6,4},{7,5},{8,10},{9,11},{10,... | collective-permute-start | bytes 393224 | tf_op jit(solution)/shard_map/ppermute | solution.py:127
  214.1 19.3 %collective-permute-start.3 = (bf16[3,2,256,128]{3,2,1,0:T(8,128)(2,1)}, bf16[3,2,256,128]{3,2,1,0:T(8,128)(2,1)}, u32[]{:S(2)}, u32[]{:S(2)}) collective-permute-start(bf16[3,2,256,128]{3,2,1,0:T(8,128)(2,1)} %get-tuple-element.57), channel_id=1, source_target_pairs={{0,1},{1,0},{2,3},{3,2},{4,5},{5,4},{6,7},{7,6},{8,9},{9,8},{10,11... | collective-permute-start | bytes 1179656 | tf_op jit(solution)/shard_map/ppermute | solution.py:127
  216.1 35.1 %collective-permute-start.4 = (bf16[3,2,256,128]{3,2,1,0:T(8,128)(2,1)}, bf16[3,2,256,128]{3,2,1,0:T(8,128)(2,1)}, u32[]{:S(2)}, u32[]{:S(2)}) collective-permute-start(bf16[3,2,256,128]{3,2,1,0:T(8,128)(2,1)} %get-tuple-element.58), channel_id=1, source_target_pairs={{0,2},{1,3},{2,0},{3,1},{4,6},{5,7},{6,4},{7,5},{8,10},{9,11},{10,... | collective-permute-start | bytes 1179656 | tf_op jit(solution)/shard_map/ppermute | solution.py:127
  217.1 34.1 %collective-permute-start.5 = (bf16[3,2,256,128]{3,2,1,0:T(8,128)(2,1)}, bf16[3,2,256,128]{3,2,1,0:T(8,128)(2,1)}, u32[]{:S(2)}, u32[]{:S(2)}) collective-permute-start(bf16[3,2,256,128]{3,2,1,0:T(8,128)(2,1)} %get-tuple-element.59), channel_id=1, source_target_pairs={{0,3},{1,2},{2,1},{3,0},{4,7},{5,6},{6,5},{7,4},{8,11},{9,10},{10,... | collective-permute-start | bytes 1179656 | tf_op jit(solution)/shard_map/ppermute | solution.py:127
  220.9 1.1 copy-start.22
  222.0 1.0 copy-start.33
  231.6 1.9 copy-start.43
  231.6 3.9 %copy-start.38 = (bf16[4,2,256,128]{3,2,1,0:T(8,128)(2,1)S(1)}, bf16[4,2,256,128]{3,2,1,0:T(8,128)(2,1)}, u32[]{:S(2)}) copy-start(bf16[4,2,256,128]{3,2,1,0:T(8,128)(2,1)} %copy-done.36) | copy-start | bytes 1572868
  233.5 23.1 %collective-permute-start.17 = (bf16[1,2,256,128]{3,2,1,0:T(8,128)(2,1)S(1)}, bf16[1,2,256,128]{3,2,1,0:T(8,128)(2,1)S(1)}, u32[]{:S(2)}, u32[]{:S(2)}) collective-permute-start(bf16[1,2,256,128]{3,2,1,0:T(8,128)(2,1)S(1)} %copy-done.43), channel_id=1, source_target_pairs={{0,3},{1,2},{2,1},{3,0},{4,7},{5,6},{6,5},{7,4},{8,11},{9,10},{10,... | collective-permute-start | bytes 393224 | tf_op jit(solution)/shard_map/ppermute | solution.py:127
  235.5 15.7 %copy-start.34 = (bf16[8,2,128,128]{3,2,1,0:T(8,128)(2,1)S(1)}, bf16[8,2,128,128]{3,2,1,0:T(8,128)(2,1)}, u32[]{:S(2)}) copy-start(bf16[8,2,128,128]{3,2,1,0:T(8,128)(2,1)} %get-tuple-element.106.refs_5_) | copy-start | bytes 1572868
  235.5 15.7 %copy-start.35 = (bf16[8,2,128,128]{3,2,1,0:T(8,128)(2,1)S(1)}, bf16[8,2,128,128]{3,2,1,0:T(8,128)(2,1)}, u32[]{:S(2)}) copy-start(bf16[8,2,128,128]{3,2,1,0:T(8,128)(2,1)} %get-tuple-element.107.refs_4_) | copy-start | bytes 1572868
  235.5 15.7 %copy-start.40 = (bf16[3,2,256,128]{3,2,1,0:T(8,128)(2,1)S(1)}, bf16[3,2,256,128]{3,2,1,0:T(8,128)(2,1)}, u32[]{:S(2)}) copy-start(bf16[3,2,256,128]{3,2,1,0:T(8,128)(2,1)} %copy-done.39) | copy-start | bytes 1179652
  (1 other events, 0.7 us)
Sparse Core Ops, SparseCore 0:
  117.4 31.2 all-gather.8
  150.6 23.4 all-gather.6
  197.7 29.1 all-gather.10
